TPU v7x, 256 devices: a whole 4x4x8 slice. The times are simulated.
256 devices in a mesh: gy: 16 (over z, core), gz: 16 (over x, y).
Axes of the slice: x: 4, y: 4, z: 8, core: 2. Of those that a mesh axis runs over, the one named last changes fastest.
Arguments:
- solution: float32 [2, 32, 512, 512], P(None, 'gz', 'gy'), may hold values from -6 to 6
- residual: float32 [2, 32, 512, 512], P(None, 'gz', 'gy'), may hold values from -32 to 32
- sensitivity: bfloat16 [2, 8, 32, 512, 512], P(None, None, 'gz', 'gy'), may hold values from -2 to 2
- sampling: int32 [512, 512], replicated, may hold values from 0 to 1
Outputs:
- new_solution: float32 [2, 32, 512, 512], P(None, 'gz', 'gy')
- new_residual: float32 [2, 32, 512, 512], P(None, 'gz', 'gy')
- new_direction: float32 [2, 32, 512, 512], P(None, 'gz', 'gy')
All inputs are finite; a program needn't handle non-finite values.
Results may differ from a plain program's by a relative error of at most 0.0025.
Values sent between devices are 32-bit elements; how exact they have to be, the bound alone decides.
A program may use at most 128 MiB of HBM per device.

v0:
```python
from functools import partial
import math

import jax
import jax.numpy as jnp
from jax import lax
from jax.sharding import PartitionSpec as P

TV_EPS = 0.1
TV_WEIGHT = 0.1
TIKHONOV = 0.1


def extended(array, sides, width):
    for axis, dim in sides:
        peers, length = (lax.axis_size(axis), array.shape[dim])
        up = [(i, (i + 1) % peers) for i in range(peers - 1)]
        down = [(j, i) for i, j in up]
        last = lax.slice_in_dim(array, length - width, length, axis=dim)
        first = lax.slice_in_dim(array, 0, width, axis=dim)
        before = lax.ppermute(last, axis, up)
        after = lax.ppermute(first, axis, down)
        array = jnp.concatenate([before, array, after], axis=dim)
    return array


def factor(length):
    leading = 8 if length % 8 == 0 and length >= 64 else 1
    return (leading, length // leading)


def unit_roots(count_rows, count_cols, length, sign):
    exponent = (
        jnp.arange(count_rows, dtype=jnp.int32)[:, None]
        * jnp.arange(count_cols, dtype=jnp.int32)[None, :]
        % length
    )
    phase_angle = sign * 2.0 * math.pi / length * exponent.astype(jnp.float32)
    return (jnp.cos(phase_angle), jnp.sin(phase_angle))


def complex_contract(pattern, real_part, imag_part, cosine, sine):
    contract = partial(jnp.einsum, pattern, precision=lax.Precision.HIGHEST)
    return (
        contract(real_part, cosine) - contract(imag_part, sine),
        contract(real_part, sine) + contract(imag_part, cosine),
    )


def transform(real_part, imag_part, along_rows, inverse):
    full_shape = real_part.shape
    length = full_shape[-2] if along_rows else full_shape[-1]
    leading, trailing = factor(length)
    sign = 1.0 if inverse else -1.0
    if along_rows:
        split_shape = full_shape[:-2] + (leading, trailing, full_shape[-1])
        if inverse:
            patterns = ("...klx,lb->...kbx", "...kbx,ka->...abx")
        else:
            patterns = ("...abx,ak->...kbx", "...kbx,bl->...klx")
    else:
        split_shape = full_shape[:-1] + (leading, trailing)
        if inverse:
            patterns = ("...kl,lb->...kb", "...kb,ka->...ab")
        else:
            patterns = ("...ab,ak->...kb", "...kb,bl->...kl")
    real_part = real_part.reshape(split_shape)
    imag_part = imag_part.reshape(split_shape)
    small_cos, small_sin = unit_roots(leading, leading, leading, sign)
    large_cos, large_sin = unit_roots(trailing, trailing, trailing, sign)
    twist_cos, twist_sin = unit_roots(leading, trailing, length, sign)
    if along_rows:
        twist_cos, twist_sin = (twist_cos[:, :, None], twist_sin[:, :, None])
    if inverse:
        real_part, imag_part = complex_contract(
            patterns[0], real_part, imag_part, large_cos, large_sin
        )
        real_part, imag_part = (
            real_part * twist_cos - imag_part * twist_sin,
            real_part * twist_sin + imag_part * twist_cos,
        )
        real_part, imag_part = complex_contract(
            patterns[1], real_part, imag_part, small_cos, small_sin
        )
        real_part, imag_part = (real_part / length, imag_part / length)
    else:
        real_part, imag_part = complex_contract(
            patterns[0], real_part, imag_part, small_cos, small_sin
        )
        real_part, imag_part = (
            real_part * twist_cos - imag_part * twist_sin,
            real_part * twist_sin + imag_part * twist_cos,
        )
        real_part, imag_part = complex_contract(
            patterns[1], real_part, imag_part, large_cos, large_sin
        )
    return (real_part.reshape(full_shape), imag_part.reshape(full_shape))


def permute_sampling(sampling):
    row_count, col_count = sampling.shape
    row_lead, row_trail = factor(row_count)
    col_lead, col_trail = factor(col_count)
    ordered = (
        sampling.reshape(row_trail, row_lead, col_count)
        .transpose(1, 0, 2)
        .reshape(row_count, col_count)
    )
    ordered = (
        ordered.reshape(row_count, col_trail, col_lead)
        .transpose(0, 2, 1)
        .reshape(row_count, col_count)
    )
    return ordered.astype(jnp.float32)


def body(solution, residual, sensitivity, sampling):
    slab_size = solution.shape[1]
    local_rows = solution.shape[2]
    fields = jnp.concatenate([solution, residual], axis=0)
    padded = extended(fields, (("gy", 2), ("gz", 1)), 1)
    centre_cells = padded[:, : slab_size + 1, : local_rows + 1, :]
    z_ahead = padded[:, 1:, : local_rows + 1, :] - centre_cells
    y_ahead = padded[:, : slab_size + 1, 1:, :] - centre_cells
    x_ahead = jnp.concatenate(
        [centre_cells[..., 1:] - centre_cells[..., :-1], jnp.zeros_like(centre_cells[..., :1])],
        axis=3,
    )
    z_global = lax.axis_index("gz") * slab_size - 1 + jnp.arange(slab_size + 1, dtype=jnp.int32)
    y_global = lax.axis_index("gy") * local_rows - 1 + jnp.arange(local_rows + 1, dtype=jnp.int32)
    z_keep = ((z_global >= 0) & (z_global < slab_size * lax.axis_size("gz") - 1)).astype(
        jnp.float32
    )
    y_keep = ((y_global >= 0) & (y_global < local_rows * lax.axis_size("gy") - 1)).astype(
        jnp.float32
    )
    z_ahead = z_ahead * z_keep[None, :, None, None]
    y_ahead = y_ahead * y_keep[None, None, :, None]
    squares = jnp.sum(
        z_ahead[:2] * z_ahead[:2] + y_ahead[:2] * y_ahead[:2] + x_ahead[:2] * x_ahead[:2], axis=0
    )
    weight = 1.0 / jnp.sqrt(squares + TV_EPS * TV_EPS)
    flux_z = weight * z_ahead[2:]
    flux_y = weight * y_ahead[2:]
    flux_cols = (weight * x_ahead[2:])[:, 1:, 1:, :]
    smooth = flux_z[:, :slab_size, 1:, :] - flux_z[:, 1:, 1:, :]
    smooth = smooth + flux_y[:, 1:, :local_rows, :] - flux_y[:, 1:, 1:, :]
    smooth = (
        smooth
        + jnp.concatenate([jnp.zeros_like(flux_cols[..., :1]), flux_cols[..., :-1]], axis=3)
        - flux_cols
    )
    coil_maps = sensitivity.astype(jnp.float32)
    coil_count = coil_maps.shape[1]
    merged_shape = (coil_count * slab_size, local_rows, solution.shape[3])
    coil_real = (coil_maps[0] * residual[0][None] - coil_maps[1] * residual[1][None]).reshape(
        merged_shape
    )
    coil_imag = (coil_maps[0] * residual[1][None] + coil_maps[1] * residual[0][None]).reshape(
        merged_shape
    )
    taken = permute_sampling(sampling)
    plane_real, plane_imag = (
        lax.all_to_all(coil_real, "gy", split_axis=0, concat_axis=1, tiled=True),
        lax.all_to_all(coil_imag, "gy", split_axis=0, concat_axis=1, tiled=True),
    )
    plane_real, plane_imag = transform(plane_real, plane_imag, False, False)
    plane_real, plane_imag = transform(plane_real, plane_imag, True, False)
    plane_real, plane_imag = (plane_real * taken, plane_imag * taken)
    plane_real, plane_imag = transform(plane_real, plane_imag, True, True)
    plane_real, plane_imag = transform(plane_real, plane_imag, False, True)
    back_real, back_imag = (
        lax.all_to_all(plane_real, "gy", split_axis=1, concat_axis=0, tiled=True),
        lax.all_to_all(plane_imag, "gy", split_axis=1, concat_axis=0, tiled=True),
    )
    back_real = back_real.reshape(coil_maps.shape[1:])
    back_imag = back_imag.reshape(coil_maps.shape[1:])
    image_real = jnp.sum(coil_maps[0] * back_real + coil_maps[1] * back_imag, axis=0)
    image_imag = jnp.sum(coil_maps[0] * back_imag - coil_maps[1] * back_real, axis=0)
    applied = jnp.stack([image_real, image_imag]) - TV_WEIGHT * smooth + TIKHONOV * residual
    norm_old = lax.psum(jnp.sum(residual * residual), ("gy", "gz"))
    curvature = lax.psum(jnp.sum(residual * applied), ("gy", "gz"))
    alpha = norm_old / curvature
    new_residual = residual - alpha * applied
    norm_new = lax.psum(jnp.sum(new_residual * new_residual), ("gy", "gz"))
    new_direction = new_residual + norm_new / norm_old * residual
    return (solution + alpha * residual, new_residual, new_direction)


def solution(mesh):
    placed = (
        P(None, "gz", "gy", None),
        P(None, "gz", "gy", None),
        P(None, None, "gz", "gy", None),
        P(),
    )
    return jax.shard_map(
        body,
        mesh=mesh,
        in_specs=placed,
        out_specs=(P(None, "gz", "gy", None), P(None, "gz", "gy", None), P(None, "gz", "gy", None)),
        check_vma=False,
    )
```

profile of v0, /device:TPU:1, one launch (start us, length us, event | category | flops | bytes accessed | tf_op | source)
XLA Modules:
  0.0 365.6 jit_solution(3809314423277586290)
XLA Ops:
  0.6 1.5 fusion.306
  3.5 38.6 %all_to_all.16 = f32[16,32,512]{2,1,0:T(8,128)} all-to-all(f32[16,32,512]{2,1,0:T(8,128)S(1)} %get-tuple-element.13), channel_id=1, replica_groups=mesh['gy'=16,'gz'=16] {'gy'}, dimensions={0} | all-to-all | bytes 2097152 | tf_op jit(solution)/shard_map/all_to_all | solution.py:164
  42.0 4.2 %all-to-all-start.1 = ((f32[16,32,512]{2,1,0:T(8,128)}), f32[16,32,512]{2,1,0:T(8,128)}, u32[]{:S(2)}, u32[]{:S(2)}) async-start(f32[16,32,512]{2,1,0:T(8,128)} %get-tuple-element.12), calls=%async_computation.1 | async-start | bytes 2097152 | tf_op jit(solution)/shard_map/all_to_all | solution.py:165
  49.3 2.3 copy.180
  52.1 2.7 reshape.383
  54.8 2.6 copy.159
  57.4 2.0 fusion.126
  59.4 2.0 fusion.133
  61.4 11.5 %all-to-all-done.1 = f32[16,32,512]{2,1,0:T(8,128)} async-done(((f32[16,32,512]{2,1,0:T(8,128)}), f32[16,32,512]{2,1,0:T(8,128)}, u32[]{:S(2)}, u32[]{:S(2)}) %all-to-all-start.1) | async-done | bytes 1048608 | tf_op jit(solution)/shard_map/all_to_all | solution.py:165
  72.9 2.9 reshape.384
  75.8 2.7 copy.160
  81.0 2.7 fusion.42
  83.7 1.7 fusion.44
  85.5 1.8 convolution_subtract_fusion.6
  87.3 1.7 reshape.409
  89.1 2.6 copy.168
  91.7 2.0 fusion.130
  93.7 2.4 fusion.123
  96.1 1.8 convolution_add_fusion.6
  97.9 1.7 reshape.410
  99.7 2.7 copy.172
  104.9 1.7 fusion.36
  106.6 1.7 fusion.38
  108.2 1.7 fusion.13
  112.4 1.7 fusion.15
  116.7 2.5 fusion.30
  120.7 1.5 fusion.5
  122.3 2.3 copy.207
  124.6 2.1 reshape.411
  126.7 2.2 fusion.75
  128.9 2.2 fusion.60
  134.3 2.6 convolution_subtract_fusion.1
  136.9 1.6 multiply_add_fusion
  140.0 1.5 fusion.3
  142.4 1.9 copy.196
  144.4 4.4 %all-to-all-start.2 = ((f32[1,512,512]{2,0,1:T(1,128)}), f32[1,512,512]{2,0,1:T(1,128)}, u32[]{:S(2)}, u32[]{:S(2)}) async-start(f32[1,512,512]{2,0,1:T(1,128)} %copy.196), calls=%async_computation.2 | async-start | bytes 2097152 | tf_op jit(solution)/shard_map/all_to_all | solution.py:173
  148.8 2.9 collective-permute-start
  151.8 1.9 collective-permute-start.1
  155.2 1.5 fusion.1
  157.3 1.9 copy.200
  159.3 16.9 %all-to-all-done.2 = f32[1,512,512]{2,0,1:T(1,128)} async-done(((f32[1,512,512]{2,0,1:T(1,128)}), f32[1,512,512]{2,0,1:T(1,128)}, u32[]{:S(2)}, u32[]{:S(2)}) %all-to-all-start.2) | async-done | bytes 1048608 | tf_op jit(solution)/shard_map/all_to_all | solution.py:173
  176.1 4.2 %all-to-all-start.3 = ((f32[1,512,512]{2,0,1:T(1,128)}), f32[1,512,512]{2,0,1:T(1,128)}, u32[]{:S(2)}, u32[]{:S(2)}) async-start(f32[1,512,512]{2,0,1:T(1,128)} %copy.200), calls=%async_computation.3 | async-start | bytes 2097152 | tf_op jit(solution)/shard_map/all_to_all | solution.py:174
  181.4 3.9 %collective-permute-start.3 = (f32[4,1,34,512]{3,2,1,0:T(8,128)}, f32[4,1,34,512]{3,2,1,0:T(8,128)}, u32[]{:S(2)}, u32[]{:S(2)}) collective-permute-start(f32[4,1,34,512]{3,2,1,0:T(8,128)} %get-tuple-element.27), channel_id=1, source_target_pairs={{0,1},{1,2},{2,3},{3,4},{4,5},{5,6},{6,7},{7,8},{8,9},{9,10},{10,1... | collective-permute-start | bytes 835592 | tf_op jit(solution)/shard_map/ppermute | solution.py:21
  187.1 5.3 %collective-permute-done.3 = f32[4,1,34,512]{3,2,1,0:T(8,128)} collective-permute-done((f32[4,1,34,512]{3,2,1,0:T(8,128)}, f32[4,1,34,512]{3,2,1,0:T(8,128)}, u32[]{:S(2)}, u32[]{:S(2)}) %collective-permute-start.3) | collective-permute-done | bytes 278560 | tf_op jit(solution)/shard_map/ppermute | solution.py:21
  194.0 3.5 collective-permute-done.2
  202.1 5.8 %all-to-all-done.3 = f32[1,512,512]{2,0,1:T(1,128)} async-done(((f32[1,512,512]{2,0,1:T(1,128)}), f32[1,512,512]{2,0,1:T(1,128)}, u32[]{:S(2)}, u32[]{:S(2)}) %all-to-all-start.3) | async-done | bytes 1048608 | tf_op jit(solution)/shard_map/all_to_all | solution.py:174
  211.4 75.9 %all-reduce.2 = (f32[]{:T(128)}, f32[]{:T(128)}) all-reduce(f32[]{:T(128)} %get-tuple-element.6, f32[]{:T(128)} %get-tuple-element.5), channel_id=1, replica_groups=mesh['gy'=16,'gz'=16] {'gy','gz'}, use_global_device_ids=true, to_apply=%region_1.2 | all-reduce | flops 2 | bytes 16 | tf_op jit(solution)/shard_map/psum | solution.py:181
  289.4 73.5 %psum.23 = f32[]{:T(128)} all-reduce(f32[]{:T(128)} %get-tuple-element.9), channel_id=1, replica_groups=mesh['gy'=16,'gz'=16] {'gy','gz'}, use_global_device_ids=true, to_apply=%region_8.9 | all-reduce | flops 1 | bytes 8 | tf_op jit(solution)/shard_map/psum | solution.py:185
  (91 shorter events, 38.0 us)
Async XLA Ops:
  0.6 1.5 copy-start.3
  3.5 43.1 %copy-start.16 = (s32[512,512]{1,0:T(8,128)S(1)}, s32[512,512]{1,0:T(8,128)}, u32[]{:S(2)}) copy-start(s32[512,512]{1,0:T(8,128)} %param.7) | copy-start | bytes 3145732
  42.0 30.9 %all-to-all-start.1 = ((f32[16,32,512]{2,1,0:T(8,128)}), f32[16,32,512]{2,1,0:T(8,128)}, u32[]{:S(2)}, u32[]{:S(2)}) async-start(f32[16,32,512]{2,1,0:T(8,128)} %get-tuple-element.12), calls=%async_computation.1 | async-start | bytes 2097152 | tf_op jit(solution)/shard_map/all_to_all | solution.py:165
  75.8 2.7 copy-start.7
  78.5 1.2 copy-start.9
  91.7 4.4 %copy-start.5 = (f32[512,8,64]{0,2,1:T(8,128)S(1)}, f32[512,8,64]{0,2,1:T(8,128)}, u32[]{:S(2)}) copy-start(f32[512,8,64]{0,2,1:T(8,128)} %fusion.42) | copy-start | bytes 3145732
  99.7 2.7 copy-start.8
  102.4 1.2 copy-start.10
  126.7 4.4 %copy-start.6 = (f32[8,64,512]{2,0,1:T(8,128)S(1)}, f32[8,64,512]{2,0,1:T(8,128)}, u32[]{:S(2)}) copy-start(f32[8,64,512]{2,0,1:T(8,128)} %fusion.30) | copy-start | bytes 3145732
  134.3 2.6 copy-start.4
  144.4 4.4 %copy-start.17 = (f32[2,2,32,512]{3,2,1,0:T(8,128)S(1)}, f32[2,2,32,512]{3,2,1,0:T(8,128)}, u32[]{:S(2)}) copy-start(f32[2,2,32,512]{3,2,1,0:T(8,128)} %param.4) | copy-start | bytes 786436
  144.4 31.8 %all-to-all-start.2 = ((f32[1,512,512]{2,0,1:T(1,128)}), f32[1,512,512]{2,0,1:T(1,128)}, u32[]{:S(2)}, u32[]{:S(2)}) async-start(f32[1,512,512]{2,0,1:T(1,128)} %copy.196), calls=%async_computation.2 | async-start | bytes 2097152 | tf_op jit(solution)/shard_map/all_to_all | solution.py:173
  148.8 31.6 %copy-start.1 = (f32[4,2,32,512]{3,2,1,0:T(8,128)}, f32[4,2,32,512]{3,2,1,0:T(8,128)S(1)}, u32[]{:S(2)}) copy-start(f32[4,2,32,512]{3,2,1,0:T(8,128)S(1)} %constant_dynamic-update-slice_fusion) | copy-start | bytes 1572868
  148.8 31.6 %collective-permute-start = (f32[4,2,1,512]{3,2,1,0:T(1,128)S(1)}, f32[4,2,1,512]{3,2,1,0:T(1,128)S(1)}, u32[]{:S(2)}, u32[]{:S(2)}) collective-permute-start(f32[4,2,1,512]{3,2,1,0:T(1,128)S(1)} %get-tuple-element.28), channel_id=1, source_target_pairs={{0,16},{16,32},{32,48},{48,64},{64,80},{80,96},{96,112},{112,128},... | collective-permute-start | bytes 49160 | tf_op jit(solution)/shard_map/ppermute | solution.py:21
  151.8 28.6 %collective-permute-start.1 = (f32[4,2,1,512]{3,2,1,0:T(1,128)S(1)}, f32[4,2,1,512]{3,2,1,0:T(1,128)S(1)}, u32[]{:S(2)}, u32[]{:S(2)}) collective-permute-start(f32[4,2,1,512]{3,2,1,0:T(1,128)S(1)} %get-tuple-element.29), channel_id=1, source_target_pairs={{16,0},{32,16},{48,32},{64,48},{80,64},{96,80},{112,96},{128,112},... | collective-permute-start | bytes 49160 | tf_op jit(solution)/shard_map/ppermute | solution.py:22
  159.3 26.1 %copy-start = (bf16[2,8,2,32,512]{4,3,2,1,0:T(8,128)(2,1)S(1)}, bf16[2,8,2,32,512]{4,3,2,1,0:T(8,128)(2,1)}, u32[]{:S(2)}) copy-start(bf16[2,8,2,32,512]{4,3,2,1,0:T(8,128)(2,1)} %param.6) | copy-start | bytes 3145732
  176.1 31.7 %all-to-all-start.3 = ((f32[1,512,512]{2,0,1:T(1,128)}), f32[1,512,512]{2,0,1:T(1,128)}, u32[]{:S(2)}, u32[]{:S(2)}) async-start(f32[1,512,512]{2,0,1:T(1,128)} %copy.200), calls=%async_computation.3 | async-start | bytes 2097152 | tf_op jit(solution)/shard_map/all_to_all | solution.py:174
  181.4 10.9 %collective-permute-start.3 = (f32[4,1,34,512]{3,2,1,0:T(8,128)}, f32[4,1,34,512]{3,2,1,0:T(8,128)}, u32[]{:S(2)}, u32[]{:S(2)}) collective-permute-start(f32[4,1,34,512]{3,2,1,0:T(8,128)} %get-tuple-element.27), channel_id=1, source_target_pairs={{0,1},{1,2},{2,3},{3,4},{4,5},{5,6},{6,7},{7,8},{8,9},{9,10},{10,1... | collective-permute-start | bytes 835592 | tf_op jit(solution)/shard_map/ppermute | solution.py:21
  185.6 11.8 %copy-start.2 = (f32[4,2,32,512]{3,2,1,0:T(8,128)S(1)}, f32[4,2,32,512]{3,2,1,0:T(8,128)}, u32[]{:S(2)}) copy-start(f32[4,2,32,512]{3,2,1,0:T(8,128)} %copy-done.1) | copy-start | bytes 1572868
  185.7 11.8 %collective-permute-start.2 = (f32[4,1,34,512]{3,2,1,0:T(8,128)}, f32[4,1,34,512]{3,2,1,0:T(8,128)S(1)}, u32[]{:S(2)}, u32[]{:S(2)}) collective-permute-start(f32[4,1,34,512]{3,2,1,0:T(8,128)} %get-tuple-element.26), channel_id=1, source_target_pairs={{1,0},{2,1},{3,2},{4,3},{5,4},{6,5},{7,6},{8,7},{9,8},{10,9},{11,1... | collective-permute-start | bytes 835592 | tf_op jit(solution)/shard_map/ppermute | solution.py:22
  199.3 0.8 copy-start.11
  209.2 1.0 copy-start.12
  209.2 1.2 copy-start.13
  209.2 1.3 copy-start.14
  209.2 1.4 copy-start.15
  209.8 154.5 %copy-start.18 = (f32[2,2,32,512]{3,2,1,0:T(8,128)S(1)}, f32[2,2,32,512]{3,2,1,0:T(8,128)}, u32[]{:S(2)}) copy-start(f32[2,2,32,512]{3,2,1,0:T(8,128)} %param.4) | copy-start | bytes 786436
  289.4 75.8 %copy-start.19 = (f32[2,2,32,512]{3,2,1,0:T(8,128)}, f32[2,2,32,512]{3,2,1,0:T(8,128)S(1)}, u32[]{:S(2)}) copy-start(f32[2,2,32,512]{3,2,1,0:T(8,128)S(1)} %get-tuple-element.10) | copy-start | bytes 786436
where the time goes:
time: 373 us; the launch traced here: 366 us
  blocking collectives  188 us (50%)
  matrix products  54.7 us (15%)
  local copies, waits for them, and re-layouts  44.3 us (12%)
  waiting for transfers between devices  42.9 us (12%)
  starting transfers between devices  23 us (6%)
  other arithmetic  8.2 us (2%)
  between operations  4.42 us (1%)
    psum x1, blocking collectives, body(): norm_old = lax.psum(jnp.sum(residual * residual), ('gy', 'gz'))  75.9 us
    psum x1, blocking collectives, body(): norm_new = lax.psum(jnp.sum(new_residual * new_residual), ('gy', 'gz'))  73.5 us
    all_to_all x1, blocking collectives, body(): lax.all_to_all(coil_real, 'gy', split_axis=0, concat_axis=1, tiled=True)  38.6 us
    another operation x12, local copies, waits for them, and re-layouts  25.7 us
    all_to_all x1, waiting for transfers between devices, body(): lax.all_to_all(plane_real, 'gy', split_axis=1, concat_axis=0, tiled=True)  16.9 us
    dot_general x8, matrix products, complex_contract(): contract(real_part, sine) + contract(imag_part, cosine)  16.2 us
    dot_general x8, matrix products, complex_contract(): contract(real_part, cosine) - contract(imag_part, sine)  13.9 us
    dot_general x8, matrix products, complex_contract(): contract(imag_part, sine)  12.9 us
  transfers between devices with their start and end apart: 7, of which 5 were waited for; matrix products, arithmetic and copies ran while one was open for 7% of the time, Pallas kernels for 0%

commit v1 on v0

v1 whole, which is shorter than its diff:
```python
import functools

import jax
import jax.numpy as jnp
import ml_dtypes
import numpy as np
from jax import lax
from jax.experimental import pallas as pl
from jax.experimental.pallas import tpu as pltpu
from jax.sharding import PartitionSpec as P

TV_EPS = 0.1
TV_WEIGHT = 0.1
TIKHONOV = 0.1
MESH = pl.DeviceIdType.MESH
F32 = jnp.float32
BF16 = jnp.bfloat16
LANES = 128
NX = 4


def split(x):
    high = x.astype(BF16)
    return high, (x - high.astype(F32)).astype(BF16)


def dot(a, b):
    return jnp.dot(a, b, preferred_element_type=F32)


def dot3(ah, al, bh, bl):
    return dot(ah, bh) + (dot(ah, bl) + dot(al, bh))


def total(x):
    rows = jnp.sum(x, axis=0, keepdims=True)
    n = rows.shape[1] // LANES
    return functools.reduce(jnp.add, [rows[:, i * LANES : (i + 1) * LANES] for i in range(n)])


def interleave(a, b):
    parts = []
    for i in range(a.shape[1] // LANES):
        parts += [a[:, i * LANES : (i + 1) * LANES], b[:, i * LANES : (i + 1) * LANES]]
    return jnp.concatenate(parts, axis=1)


def kernel(
    n, m, sol, res, sens, samp_in, g_in,
    out_app, out_scal,
    sbuf, relay, srecv, xrel, xall, vh, vl, yh, yl, samp, g,
    part, pair, tot, gath, fin, image, smooth,
    hz, hy_s, hy, qz_s, qz, qy_s, qy, ps1_s, ps1, ps2_s, ps2,
    csem, xls, xlr, zs, zr, xrs, xrr, xzs, xar, ms, os,
    prs, prr, gs, gr, fs, fr, hs, hr, p1s, p1r, p2s, p2r,
):
    y = lax.axis_index("gy")
    w = lax.axis_index("gz")
    z, core = y // 2, lax.rem(y, 2)
    x, yy = w // NX, lax.rem(w, NX)
    nz = n // 2
    slab, rows, cols = res.shape[1:]
    sib = 1 - core
    pos = (x, yy)
    odd = lax.rem(z, 2)
    lp = (1 - odd) * x + odd * yy
    sp = z // 2
    l = 2 * lp + core
    line = 2 * NX

    def dev(j, p, z_, core_):
        return (2 * z_ + core_, NX * x + p if j else NX * p + yy)

    def on_line(p, z_, core_):
        return (2 * z_ + core_, (1 - odd) * (NX * p + yy) + odd * (NX * x + p))

    def at_y(t):
        return (t, w)

    def at_z(t):
        return (y, t)

    def across(p, k):
        return (p, p + 1 - 2 * lax.rem(p, 2), lax.rem(p + 2, NX), NX - 1 - p)[k]

    def remote(src, dst, ssem, rsem, device):
        return pltpu.make_async_remote_copy(
            src_ref=src, dst_ref=dst, send_sem=ssem, recv_sem=rsem, device_id=device, device_id_type=MESH
        )

    def loop(lo, hi, f):
        def step(i, c):
            f(i)
            return c

        lax.fori_loop(lo, hi, step, 0)

    barrier = pltpu.get_barrier_semaphore()

    def hail(device):
        pl.semaphore_signal(barrier, inc=1, device_id=device, device_id_type=MESH)

    loop(1, n, lambda k: hail(at_y(lax.rem(y + k, n))))
    loop(1, m, lambda k: hail(at_z(lax.rem(w + k, m))))
    for j in range(slab):
        loop(1, NX, lambda k: hail(dev(j, lax.rem(pos[j] + k, NX), z, sib)))
        hail(dev(j, lax.rem(pos[j] + z, NX), slab * pos[j] + j, core))

    def from_self(j):
        return jnp.logical_and(lax.rem(z, NX) == 0, slab * pos[j] + j == z)

    loads = [
        pltpu.make_async_copy(a, b, csem.at[i]) for i, (a, b) in enumerate([(g_in, g), (samp_in, samp)])
    ]
    for c in loads:
        c.start()

    def widen(c):
        for j in range(slab):
            sbuf[c, j, 0] = sens[0, c, j].astype(F32)
            sbuf[c, j, 1] = sens[1, c, j].astype(F32)

    loop(0, line, widen)

    up_y, down_y = lax.rem(y + 1, n), lax.rem(y + n - 1, n)
    up_z, down_z = lax.rem(w + 1, m), lax.rem(w + m - 1, m)
    for f, field in enumerate((sol, res)):
        for p in range(2):
            for s in range(slab):
                i = f * 2 * slab + p * slab + s
                hy_s[i : i + 1, :] = field[p, s, 0:1, :]

    pl.semaphore_wait(barrier, n + m - 2 + slab * NX)

    moved = lax.rem(z, NX) != 0

    def res_over(j):
        return remote(res.at[:, j], xrel.at[j], xrs.at[j], xrr.at[j], dev(j, lax.rem(pos[j] + z, NX), z, core))

    for j in range(slab):
        @pl.when(moved)
        def _():
            res_over(j).start()

        @pl.when(jnp.logical_not(moved))
        def _():
            xrel[j] = res[:, j]

    steps = [(0, 1), (1, 0), (3, 0), (1, 1), (3, 1), (2, 0), (2, 1)]

    def partner(j, step):
        p = across(pos[j], step[0])
        c = sib if step[1] else core
        return p, c, 2 * p + c

    def maps_over(j, step):
        p, c, t = partner(j, step)
        me = 2 * pos[j] + core
        return remote(sbuf.at[t, j], relay.at[j, me], xls.at[line * j + t], xlr.at[line * j + me], dev(j, p, z, c))

    for step in steps:
        for j in range(slab):
            maps_over(j, step).start()

    halo1 = [
        remote(sol.at[:, 0], hz.at[0], hs.at[0], hr.at[0], at_z(down_z)),
        remote(res.at[:, 0], hz.at[1], hs.at[1], hr.at[1], at_z(down_z)),
        remote(hy_s, hy, hs.at[2], hr.at[2], at_y(down_y)),
    ]
    for h in halo1:
        h.start()

    def pass_on(src, j, t):
        zt = slab * (t // 2) + j
        slot = 2 * z + lax.rem(t, 2)
        cp = remote(src, srecv.at[slot], zs.at[line * j + t], zr.at[slot], dev(0, x, zt, core))
        return zt, slot, cp

    def forward_maps(src, j, t):
        zt, slot, cp = pass_on(src, j, t)

        @pl.when(zt != z)
        def _():
            cp.start()

        @pl.when(zt == z)
        def _():
            srecv[slot] = src[...]

    for j in range(slab):
        t = 2 * pos[j] + core
        forward_maps(sbuf.at[t, j], j, t)

    def forward_res(j):
        zt = slab * lax.rem(pos[j] + NX - lax.rem(z, NX), NX) + j
        return zt, remote(xrel.at[j], xall.at[y], xzs.at[j], xar.at[y], dev(0, x, zt, core))

    for j in range(slab):
        @pl.when(moved)
        def _():
            res_over(j).wait_recv()

        zt, cp = forward_res(j)

        @pl.when(zt != z)
        def _():
            cp.start()

        @pl.when(zt == z)
        def _():
            xall[y] = xrel[j]

    def relay_maps(step):
        for j in range(slab):
            _, _, t = partner(j, step)
            remote(sbuf.at[t, j], relay.at[j, t], xls.at[line * j + t], xlr.at[line * j + t], dev(j, pos[j], z, sib)).wait_recv()
            forward_maps(relay.at[j, t], j, t)

    for step in steps[:3]:
        relay_maps(step)

    first = lax.rem(lp + NX - lax.rem(sp, NX), NX)

    def hand(slot, i, k):
        p = lax.rem(lp + k, NX)
        return remote(xall.at[slot], xall.at[slot], ms.at[i * NX + k], xar.at[slot], on_line(p, z, core))

    def to_other(zz):
        slot = 2 * zz + core
        return remote(xall.at[slot], xall.at[slot], os.at[zz], xar.at[slot], on_line(lp, z, sib))

    for i in range(nz // NX):
        zz = first + NX * i
        slot = 2 * zz + core

        @pl.when(zz != z)
        def _():
            remote(xrel.at[0], xall.at[slot], xzs.at[0], xar.at[slot], dev(0, x, zz, core)).wait_recv()

        for k in range(1, NX):
            hand(slot, i, k).start()
        to_other(zz).start()

    for step in steps[3:]:
        relay_maps(step)

    for h in halo1:
        h.wait_recv()
    row = lax.broadcasted_iota(jnp.int32, (rows, cols), 0)
    col = lax.broadcasted_iota(jnp.int32, (rows, cols), 1)
    keep_y = jnp.logical_or(row < rows - 1, y < n - 1)
    keep_z = jnp.full((rows, cols), w, jnp.int32) < m - 1

    def ahead(f, field, p, s):
        v = field[p, s]
        dx = jnp.where(col == cols - 1, 0.0, pltpu.roll(v, cols - 1, 1) - v)
        i = f * 2 * slab + p * slab + s
        nxt = jnp.where(row == rows - 1, jnp.broadcast_to(hy[i : i + 1, :], (rows, cols)), pltpu.roll(v, rows - 1, 0))
        dy = jnp.where(keep_y, nxt - v, 0.0)
        if s + 1 < slab:
            dz = field[p, s + 1] - v
        else:
            dz = jnp.where(keep_z, hz[f, p] - v, 0.0)
        return dx, dy, dz

    qy_s[...] = jnp.zeros_like(qy_s)
    for s in range(slab):
        sq = jnp.zeros((rows, cols), F32)
        for p in range(2):
            for d in ahead(0, sol, p, s):
                sq = sq + d * d
        weight = 1.0 / jnp.sqrt(sq + TV_EPS * TV_EPS)
        for p in range(2):
            dx, dy, dz = (weight * d for d in ahead(1, res, p, s))
            before_x = jnp.where(col == 0, 0.0, pltpu.roll(dx, 1, 1))
            before_y = jnp.where(row == 0, 0.0, pltpu.roll(dy, 1, 0))
            here = (before_x - dx) + (before_y - dy) - dz
            if s > 0:
                here = here + qz_s[p]
            smooth[p, s] = here
            qz_s[p] = dz
            i = p * slab + s
            qy_s[i : i + 1, :] = dy[rows - 1 : rows, :]
    halo2 = [
        remote(qz_s, qz, hs.at[3], hr.at[3], at_z(up_z)),
        remote(qy_s, qy, hs.at[4], hr.at[4], at_y(up_y)),
    ]
    for h in halo2:
        h.start()

    for k in range(1, NX):
        for i in range(nz // NX):
            zz = lax.rem(first + k, NX) + NX * i
            slot = 2 * zz + core
            remote(xall.at[slot], xall.at[slot], ms.at[0], xar.at[slot], on_line(lax.rem(lp + k, NX), z, core)).wait_recv()
            to_other(zz).start()

    per = 4
    tile = per * rows
    groups = n // per
    loads[0].wait()

    def ready(s):
        zz = s // 2

        @pl.when(zz != z)
        def _():
            remote(relay.at[0, 0], srecv.at[s], zs.at[0], zr.at[s], dev(0, x, zz, core)).wait_recv()

        @pl.when(lax.rem(s, 2) == sib)
        def _():
            remote(xall.at[s], xall.at[s], os.at[0], xar.at[s], on_line(lp, z, sib)).wait_recv()

    def forward_cols(i):
        q = lax.rem(y // per + groups - 1 - i, groups)
        for t in range(per):
            ready(q * per + t)
        block = []
        for t in range(per):
            sr, si = srecv[q * per + t, 0], srecv[q * per + t, 1]
            xr, xi = xall[q * per + t, 0], xall[q * per + t, 1]
            block.append(interleave(sr * xr - si * xi, -(sr * xi + si * xr)))
        ah, al = split(jnp.concatenate(block, axis=0))
        v = dot3(ah, al, g[0], g[1])
        at = pl.ds(pl.multiple_of(q * tile, tile), tile)
        vh[0, at], vl[0, at] = split(v[:, :cols])
        vh[1, at], vl[1, at] = split(-v[:, cols:])

    loop(0, groups, forward_cols)

    full = n * rows
    loads[1].wait()
    scale = 1.0 / (full * cols)

    def forward_rows(t):
        at = pl.ds(pl.multiple_of(2 * t * tile, 2 * tile), 2 * tile)
        h, l_ = g[0, at], g[1, at]
        v = dot3(h[:, :full], l_[:, :full], vh[0], vl[0]) + dot3(h[:, full:], l_[:, full:], vh[1], vl[1])
        k = pl.ds(pl.multiple_of(t * tile, tile), tile)
        taken = samp[k].astype(F32) * scale
        yh[0, k], yl[0, k] = split(v[:tile] * taken)
        yh[1, k], yl[1, k] = split(v[tile:] * -taken)

    loop(0, groups, forward_rows)

    def to_sib(zz):
        return remote(part.at[2 * zz + sib], pair.at[zz], prs.at[zz], prr.at[zz], on_line(lp, z, sib))

    def to_adder(zz):
        t = lax.rem(sp + zz, NX)
        return t, remote(tot.at[zz], gath.at[zz // NX, lp], gs.at[zz], gr.at[NX * (zz // NX) + lp], on_line(t, z, core))

    def add_pair(zz):
        to_sib(zz).wait_recv()
        tot[zz] = part[2 * zz + core] + pair[zz]
        t, cp = to_adder(zz)

        @pl.when(t != lp)
        def _():
            cp.start()

    def home(i):
        zz = first + NX * i
        return zz, remote(fin.at[i], image.at[odd], fs.at[i], fr.at[odd], on_line(sp, zz, core))

    def add_line(i):
        zz, cp = home(i)
        v = tot[zz]
        for k in range(1, NX):
            t = lax.rem(lp + k, NX)
            remote(tot.at[zz], gath.at[i, t], gs.at[zz], gr.at[NX * i + t], on_line(t, z, core)).wait_recv()
            v = v + gath[i, t]
        here = jnp.logical_and(sp == lp, zz == z)

        @pl.when(here)
        def _():
            image[odd] = v

        @pl.when(jnp.logical_not(here))
        def _():
            fin[i] = v
            cp.start()

    def inverse(q):
        at = pl.ds(pl.multiple_of(2 * q * tile, 2 * tile), 2 * tile)
        h, l_ = g[0, at], g[1, at]
        v = dot3(h[:, :full], l_[:, :full], yh[0], yl[0]) + dot3(h[:, full:], l_[:, full:], yh[1], yl[1])
        ah, al = split(interleave(v[:tile], -v[tile:]))
        v = dot3(ah, al, g[0], g[1])
        for t in range(per):
            s = q * per + t
            vr, vi = v[t * rows : (t + 1) * rows, :cols], v[t * rows : (t + 1) * rows, cols:]
            sr, si = srecv[s, 0], srecv[s, 1]
            part[s, 0] = sr * vr + si * vi
            part[s, 1] = sr * vi - si * vr
        for t in range(per // 2):
            to_sib(q * per // 2 + t).start()

        @pl.when(q > 0)
        def _():
            for t in range(per // 2):
                add_pair((q - 1) * per // 2 + t)

        @pl.when(q == groups - 1)
        def _():
            add_line(0)

    loop(0, groups, inverse)
    for t in range(per // 2):
        add_pair((groups - 1) * per // 2 + t)
    add_line(1)

    for h in halo2:
        h.wait_recv()
    at_zero = jnp.full((rows, cols), w, jnp.int32) > 0
    at_top = jnp.logical_and(row == 0, y > 0)
    for p in range(2):
        for s in range(slab):
            i = p * slab + s
            v = smooth[p, s] + jnp.where(at_top, jnp.broadcast_to(qy[i : i + 1, :], (rows, cols)), 0.0)
            if s == 0:
                v = v + jnp.where(at_zero, qz[p], 0.0)
            smooth[p, s] = v

    rr = jnp.zeros((1, LANES), F32)
    ra = jnp.zeros((1, LANES), F32)
    aa = jnp.zeros((1, LANES), F32)
    for s in range(slab):
        @pl.when(jnp.logical_not(from_self(s)))
        def _():
            remote(fin.at[0], image.at[s], fs.at[0], fr.at[s], dev(s, lax.rem(pos[s] + z, NX), slab * pos[s] + s, core)).wait_recv()

        for p in range(2):
            r = res[p, s]
            a = image[s, p] - TV_WEIGHT * smooth[p, s] + TIKHONOV * r
            out_app[p, s] = a
            rr, ra, aa = rr + total(r * r), ra + total(r * a), aa + total(a * a)

    def exchange(send, recv, ssem, rsem, me, size, where):
        recv[me] = send[...]

        def go(k):
            t = lax.rem(me + k, size)
            remote(send, recv.at[me], ssem, rsem, where(t)).start()

        loop(1, size, go)
        others = recv.at[pl.ds(0, size - 1)]
        remote(others, others, ssem, rsem, where(lax.rem(me + 1, size))).wait_recv()
        return functools.reduce(jnp.add, [recv[i] for i in range(size)])

    ps1_s[...] = jnp.zeros_like(ps1_s)
    ps1_s[0:1, :] = rr
    ps1_s[1:2, :] = ra
    ps1_s[2:3, :] = aa
    ps2_s[...] = exchange(ps1_s, ps1, p1s, p1r, y, n, at_y)
    sums = jnp.sum(exchange(ps2_s, ps2, p2s, p2r, w, m, at_z), axis=1, keepdims=True)
    norm_old, curvature, applied2 = sums[0:1], sums[1:2], sums[2:3]
    alpha = norm_old / curvature
    norm_new = jnp.maximum(alpha * alpha * applied2 - norm_old, 0.0)
    out_scal[0:1, :] = jnp.broadcast_to(alpha, (1, cols))
    out_scal[1:2, :] = jnp.broadcast_to(norm_new / norm_old, (1, cols))

    for recv, ssem, rsem, size, there in ((ps1, p1s, p1r, n, at_y(up_y)), (ps2, p2s, p2r, m, at_z(up_z))):
        others = recv.at[pl.ds(0, size - 1)]
        remote(others, others, ssem, rsem, there).wait_send()
    for h in halo1 + halo2:
        h.wait_send()
    for j in range(slab):
        @pl.when(moved)
        def _():
            res_over(j).wait_send()

        for step in steps:
            maps_over(j, step).wait_send()

        def sent_maps(t):
            zt, _, cp = pass_on(sbuf.at[0, j], j, t)

            @pl.when(zt != z)
            def _():
                cp.wait_send()

        loop(0, line, sent_maps)
        zt, cp = forward_res(j)

        @pl.when(zt != z)
        def _():
            cp.wait_send()

    for i in range(nz // NX):
        for k in range(1, NX):
            hand(2 * (first + NX * i) + core, i, k).wait_send()
        zz, cp = home(i)

        @pl.when(jnp.logical_not(jnp.logical_and(sp == lp, zz == z)))
        def _():
            cp.wait_send()

    def sent_sums(zz):
        to_other(zz).wait_send()
        to_sib(zz).wait_send()
        t, cp = to_adder(zz)

        @pl.when(t != lp)
        def _():
            cp.wait_send()

    loop(0, nz, sent_sums)


def matrix(length, rows):
    k = np.arange(length)
    angle = 2.0 * np.pi / length * (np.outer(k, k) % length)
    c, s = np.cos(angle), np.sin(angle)
    g = np.block([[c, s], [-s, c]])
    blocks = length // rows
    g = g.reshape(2, blocks, rows, 2 * length).transpose(1, 0, 2, 3).reshape(2 * length, 2 * length)
    g = g.astype(np.float32)
    h = g.astype(ml_dtypes.bfloat16)
    return np.stack([h, (g - h.astype(np.float32)).astype(ml_dtypes.bfloat16)])


def body(n, m, solution, residual, sensitivity, sampling):
    _, slab, rows, cols = solution.shape
    coils = sensitivity.shape[1]
    full = n * rows
    g = jnp.asarray(matrix(full, LANES))
    vmem = pl.BlockSpec(memory_space=pltpu.VMEM)
    hbm = pl.BlockSpec(memory_space=pl.ANY)
    dma = pltpu.SemaphoreType.DMA
    chunk = (2, rows, cols)

    def f32(*shape):
        return pltpu.VMEM(shape, F32)

    def bf16(*shape):
        return pltpu.VMEM(shape, BF16)

    applied, scal = pl.pallas_call(
        functools.partial(kernel, n, m),
        out_shape=(jax.ShapeDtypeStruct(solution.shape, F32), jax.ShapeDtypeStruct((2, cols), F32)),
        in_specs=[vmem, vmem, vmem, hbm, hbm],
        out_specs=(vmem, vmem),
        scratch_shapes=[
            f32(coils, slab, *chunk), f32(slab, 2 * NX, *chunk), f32(n, *chunk), f32(slab, *chunk), f32(n, *chunk),
            bf16(2, full, cols), bf16(2, full, cols), bf16(2, full, cols), bf16(2, full, cols),
            pltpu.VMEM(sampling.shape, sampling.dtype), bf16(*g.shape),
            f32(n, *chunk), f32(n // 2, *chunk), f32(n // 2, *chunk), f32(n // 2 // NX, NX, *chunk), f32(2, *chunk),
            f32(slab, *chunk), f32(*solution.shape),
            f32(2, *chunk), f32(8, cols), f32(8, cols), f32(*chunk), f32(*chunk), f32(8, cols), f32(8, cols),
            f32(8, LANES), f32(n, 8, LANES), f32(8, LANES), f32(m, 8, LANES),
            dma((2,)), dma((2 * NX * slab,)), dma((2 * NX * slab,)), dma((2 * NX * slab,)), dma((n,)), dma((slab,)), dma((slab,)),
            dma((slab,)), dma((n,)), dma((n // 2 // NX * NX,)), dma((n // 2,)),
            dma((n // 2,)), dma((n // 2,)), dma((n // 2,)), dma((n // 2,)), dma((n // 2 // NX,)), dma((slab,)),
            dma((5,)), dma((5,)), dma, dma, dma, dma,
        ],
        compiler_params=pltpu.CompilerParams(
            collective_id=0, has_side_effects=True, vmem_limit_bytes=56 * 1024 * 1024
        ),
        name="iteration",
    )(solution, residual, sensitivity, sampling, g)
    alpha, beta = scal[0], scal[1]
    new_residual = residual - alpha * applied
    return solution + alpha * residual, new_residual, new_residual + beta * residual


def solution(mesh):
    n, m = mesh.shape["gy"], mesh.shape["gz"]
    field = P(None, "gz", "gy", None)
    return jax.shard_map(
        functools.partial(body, n, m),
        mesh=mesh,
        in_specs=(field, field, P(None, None, "gz", "gy", None), P()),
        out_specs=(field, field, field),
        check_vma=False,
    )
```

time: 373 us -> 133 us (0.36); the launches traced: 366 us -> 133 us
  blocking collectives: 188 us -> 0 us
  Pallas kernels: 0 us -> 130 us
  matrix products: 54.7 us -> 0 us
  local copies, waits for them, and re-layouts: 44.3 us -> 0.77 us
  waiting for transfers between devices: 42.9 us -> 0 us
  starting transfers between devices: 23 us -> 0 us
  other arithmetic: 8.2 us -> 1.91 us
  between operations: 4.42 us -> 0.66 us
    psum x2 -> x0, blocking collectives: 149 us -> none  [the longest x1 75.9 us: body(): norm_old = lax.psum(jnp.sum(residual * residual), ('gy', 'gz'))]
    pallas_call x0 -> x1, Pallas kernels: none -> 130 us  [body(): pl.pallas_call(functools.partial(kernel, n, m), out_shape=(jax.ShapeDtype...]
    dot_general x32 -> x0, matrix products: 54.7 us -> none  [the longest x8 16.2 us: complex_contract(): contract(real_part, sine) + contract(imag_part, cosine)]
    all_to_all x1 -> x0, blocking collectives: 38.6 us -> none  [body(): lax.all_to_all(coil_real, 'gy', split_axis=0, concat_axis=1, tiled=True)]
    all_to_all x3 -> x0, waiting for transfers between devices: 34.1 us -> none  [the longest x1 16.9 us: body(): lax.all_to_all(plane_real, 'gy', split_axis=1, concat_axis=0, tiled=True)]
    another operation x12 -> x0, local copies, waits for them, and re-layouts: 25.7 us -> none
    all_to_all x3 -> x0, starting transfers between devices: 12.8 us -> none  [the longest x1 4.36 us: body(): lax.all_to_all(plane_real, 'gy', split_axis=1, concat_axis=0, tiled=True)]
    ppermute x4 -> x0, starting transfers between devices: 10.2 us -> none  [the longest x2 6.84 us: extended(): before = lax.ppermute(last, axis, up)]
  transfers between devices with their start and end apart: 7 -> 0, of which waited for: 5 -> 0; matrix products, arithmetic and copies ran while one was open for 7% -> 0% of each run, Pallas kernels for 0% -> 0%
where the time goes in v1:
time: 133 us
  Pallas kernels  130 us (98%)
  other arithmetic  1.91 us (1%)
    pallas_call x1, Pallas kernels, body(): pl.pallas_call(functools.partial(kernel, n, m), out_shape=(jax.ShapeDtype...  130 us

profile of v1, /device:TPU:1, one launch (start us, length us, event | category | flops | bytes accessed | tf_op | source)
XLA Modules:
  0.0 133.0 jit_solution(8695813707554991067)
XLA Ops:
  0.6 0.0 copy-start
  0.6 0.0 copy-start.1
  0.7 129.7 %iteration.1 = (f32[2,2,32,512]{3,2,1,0:T(8,128)}, f32[2,512]{1,0:T(2,128)}) custom-call(f32[2,2,32,512]{3,2,1,0:T(8,128)} %sol.1, f32[2,2,32,512]{3,2,1,0:T(8,128)} %res.1, bf16[2,8,2,32,512]{4,3,2,1,0:T(8,128)(2,1)} %sens.1, s32[512,512]{1,0:T(8,128)} %samp_in.1, bf16[2,1024,1024]{2,1,0:T(8,128)(2,1)} %constant.2.clone.g_in), custom_call_target="tpu_custom_call" | custom-call | tf_op jit(solution)/shard_map/iteration/pallas_call | solution.py:539
  130.3 0.8 fusion
  131.1 0.0 copy-done
  131.1 0.0 copy-done.1
  131.1 1.9 %multiply_add_fusion = (f32[2,2,32,512]{3,2,1,0:T(8,128)}, f32[2,2,32,512]{3,2,1,0:T(8,128)}, f32[2,2,32,512]{3,2,1,0:T(8,128)}) fusion(f32[2,2,32,512]{3,2,1,0:T(8,128)S(1)} %copy-done, f32[512]{0:T(512)S(1)} %bitcast.2, f32[2,2,32,512]{3,2,1,0:T(8,128)} %get-tuple-element.6, f32[512]{0:T(512)S(1)} %bitcast.3, f32[2,2,32,512]{3,2,1,0:T(8,128)S(1)} %copy-done.1), kind=kLoop, calls=%fused_computation | loop fusion | flops 393216 | bytes 1576960 | tf_op jit(solution)/shard_map/add | solution.py:564
Async XLA Ops:
  0.6 130.5 %copy-start = (f32[2,2,32,512]{3,2,1,0:T(8,128)S(1)}, f32[2,2,32,512]{3,2,1,0:T(8,128)}, u32[]{:S(2)}) copy-start(f32[2,2,32,512]{3,2,1,0:T(8,128)} %res.1) | copy-start | bytes 786436
  0.6 130.5 %copy-start.1 = (f32[2,2,32,512]{3,2,1,0:T(8,128)S(1)}, f32[2,2,32,512]{3,2,1,0:T(8,128)}, u32[]{:S(2)}) copy-start(f32[2,2,32,512]{3,2,1,0:T(8,128)} %sol.1) | copy-start | bytes 786436

commit v2 on v1

--- a/solution.py
+++ b/solution.py
@@ -45,14 +45,18 @@
     return jnp.concatenate(parts, axis=1)
 
 
+def part_of(v, i):
+    return jnp.concatenate([v[:, (2 * b + i) * LANES : (2 * b + i + 1) * LANES] for b in range(v.shape[1] // LANES // 2)], axis=1)
+
+
 def kernel(
     n, m, sol, res, sens, samp_in, g_in,
-    out_app, out_scal,
-    sbuf, relay, srecv, xrel, xall, vh, vl, yh, yl, samp, g,
-    part, pair, tot, gath, fin, image, smooth,
+    out_app, out_alpha, out_beta,
+    sbuf, relay, srecv, xrel, xall, vh, vl, yacc, yh, yl, samp, g,
+    part, pair, tot, gath, fin, image, smooth, local, local_in,
     hz, hy_s, hy, qz_s, qz, qy_s, qy, ps1_s, ps1, ps2_s, ps2,
     csem, xls, xlr, zs, zr, xrs, xrr, xzs, xar, ms, os,
-    prs, prr, gs, gr, fs, fr, hs, hr, p1s, p1r, p2s, p2r,
+    prs, prr, gs, gr, fs, fr, hs, hr, ls, lr, p1s, p1r, p2s, p2r,
 ):
     y = lax.axis_index("gy")
     w = lax.axis_index("gz")
@@ -216,7 +220,7 @@
             remote(sbuf.at[t, j], relay.at[j, t], xls.at[line * j + t], xlr.at[line * j + t], dev(j, pos[j], z, sib)).wait_recv()
             forward_maps(relay.at[j, t], j, t)
 
-    for step in steps[:3]:
+    for step in steps:
         relay_maps(step)
 
     first = lax.rem(lp + NX - lax.rem(sp, NX), NX)
@@ -240,9 +244,6 @@
         for k in range(1, NX):
             hand(slot, i, k).start()
         to_other(zz).start()
-
-    for step in steps[3:]:
-        relay_maps(step)
 
     for h in halo1:
         h.wait_recv()
@@ -298,7 +299,6 @@
     per = 4
     tile = per * rows
     groups = n // per
-    loads[0].wait()
 
     def ready(s):
         zz = s // 2
@@ -311,8 +311,46 @@
         def _():
             remote(xall.at[s], xall.at[s], os.at[0], xar.at[s], on_line(lp, z, sib)).wait_recv()
 
-    def forward_cols(i):
+    at_zero = jnp.full((rows, cols), w, jnp.int32) > 0
+    at_top = jnp.logical_and(row == 0, y > 0)
+
+    def local_over(j):
+        there = dev(j, lax.rem(pos[j] + z, NX), slab * pos[j] + j, core)
+        return remote(local.at[j], local_in.at[z // NX], ls.at[j], lr.at[z // NX], there)
+
+    def send_local():
+        for h in halo2:
+            h.wait_recv()
+        for p in range(2):
+            for s in range(slab):
+                i = p * slab + s
+                v = smooth[p, s] + jnp.where(at_top, jnp.broadcast_to(qy[i : i + 1, :], (rows, cols)), 0.0)
+                if s == 0:
+                    v = v + jnp.where(at_zero, qz[p], 0.0)
+                local[s, p] = TIKHONOV * res[p, s] - TV_WEIGHT * v
+        for j in range(slab):
+            @pl.when(jnp.logical_not(from_self(j)))
+            def _():
+                local_over(j).start()
+
+            @pl.when(from_self(j))
+            def _():
+                local_in[z // NX] = local[j]
+
+    full = n * rows
+    scale = 1.0 / (full * cols)
+    yacc[...] = jnp.zeros_like(yacc)
+    loads[0].wait()
+    loads[1].wait()
+
+    def forward(i):
         q = lax.rem(y // per + groups - 1 - i, groups)
+        last = i == groups - 1
+
+        @pl.when(last)
+        def _():
+            send_local()
+
         for t in range(per):
             ready(q * per + t)
         block = []
@@ -322,26 +360,26 @@
             block.append(interleave(sr * xr - si * xi, -(sr * xi + si * xr)))
         ah, al = split(jnp.concatenate(block, axis=0))
         v = dot3(ah, al, g[0], g[1])
-        at = pl.ds(pl.multiple_of(q * tile, tile), tile)
-        vh[0, at], vl[0, at] = split(v[:, :cols])
-        vh[1, at], vl[1, at] = split(-v[:, cols:])
-
-    loop(0, groups, forward_cols)
-
-    full = n * rows
-    loads[1].wait()
-    scale = 1.0 / (full * cols)
-
-    def forward_rows(t):
-        at = pl.ds(pl.multiple_of(2 * t * tile, 2 * tile), 2 * tile)
-        h, l_ = g[0, at], g[1, at]
-        v = dot3(h[:, :full], l_[:, :full], vh[0], vl[0]) + dot3(h[:, full:], l_[:, full:], vh[1], vl[1])
-        k = pl.ds(pl.multiple_of(t * tile, tile), tile)
-        taken = samp[k].astype(F32) * scale
-        yh[0, k], yl[0, k] = split(v[:tile] * taken)
-        yh[1, k], yl[1, k] = split(v[tile:] * -taken)
-
-    loop(0, groups, forward_rows)
+        vh[:tile], vl[:tile] = split(part_of(v, 0))
+        vh[tile:], vl[tile:] = split(-part_of(v, 1))
+
+        def rows_tile(t):
+            at = pl.ds(pl.multiple_of(2 * t * tile, 2 * tile), 2 * tile)
+            k = pl.ds(pl.multiple_of(2 * q * tile, 2 * tile), 2 * tile)
+            v = yacc[at] + dot3(g[0, at, k], g[1, at, k], vh[...], vl[...])
+
+            @pl.when(jnp.logical_not(last))
+            def _():
+                yacc[at] = v
+
+            @pl.when(last)
+            def _():
+                taken = samp[pl.ds(pl.multiple_of(t * tile, tile), tile)].astype(F32) * scale
+                yh[at], yl[at] = split(v * jnp.concatenate([taken, -taken], axis=0))
+
+        loop(0, groups, rows_tile)
+
+    loop(0, groups, forward)
 
     def to_sib(zz):
         return remote(part.at[2 * zz + sib], pair.at[zz], prs.at[zz], prr.at[zz], on_line(lp, z, sib))
@@ -370,6 +408,17 @@
             t = lax.rem(lp + k, NX)
             remote(tot.at[zz], gath.at[i, t], gs.at[zz], gr.at[NX * i + t], on_line(t, z, core)).wait_recv()
             v = v + gath[i, t]
+
+        @pl.when(jnp.logical_not(jnp.logical_and(sp == lp, zz == z)))
+        def _():
+            remote(local.at[0], local_in.at[i], ls.at[0], lr.at[i], on_line(sp, zz, core)).wait_recv()
+
+        v = v + local_in[i]
+        for p in range(2):
+            a, r = v[p], xall[2 * zz + core, p]
+            ps1_s[0:1, :] += total(r * r)
+            ps1_s[1:2, :] += total(r * a)
+            ps1_s[2:3, :] += total(a * a)
         here = jnp.logical_and(sp == lp, zz == z)
 
         @pl.when(here)
@@ -383,13 +432,13 @@
 
     def inverse(q):
         at = pl.ds(pl.multiple_of(2 * q * tile, 2 * tile), 2 * tile)
-        h, l_ = g[0, at], g[1, at]
-        v = dot3(h[:, :full], l_[:, :full], yh[0], yl[0]) + dot3(h[:, full:], l_[:, full:], yh[1], yl[1])
+        v = dot3(g[0, at], g[1, at], yh[...], yl[...])
         ah, al = split(interleave(v[:tile], -v[tile:]))
         v = dot3(ah, al, g[0], g[1])
+        re, im = part_of(v, 0), part_of(v, 1)
         for t in range(per):
             s = q * per + t
-            vr, vi = v[t * rows : (t + 1) * rows, :cols], v[t * rows : (t + 1) * rows, cols:]
+            vr, vi = re[t * rows : (t + 1) * rows], im[t * rows : (t + 1) * rows]
             sr, si = srecv[s, 0], srecv[s, 1]
             part[s, 0] = sr * vr + si * vi
             part[s, 1] = sr * vi - si * vr
@@ -405,37 +454,12 @@
         def _():
             add_line(0)
 
+    ps1_s[...] = jnp.zeros_like(ps1_s)
     loop(0, groups, inverse)
     for t in range(per // 2):
         add_pair((groups - 1) * per // 2 + t)
     add_line(1)
 
-    for h in halo2:
-        h.wait_recv()
-    at_zero = jnp.full((rows, cols), w, jnp.int32) > 0
-    at_top = jnp.logical_and(row == 0, y > 0)
-    for p in range(2):
-        for s in range(slab):
-            i = p * slab + s
-            v = smooth[p, s] + jnp.where(at_top, jnp.broadcast_to(qy[i : i + 1, :], (rows, cols)), 0.0)
-            if s == 0:
-                v = v + jnp.where(at_zero, qz[p], 0.0)
-            smooth[p, s] = v
-
-    rr = jnp.zeros((1, LANES), F32)
-    ra = jnp.zeros((1, LANES), F32)
-    aa = jnp.zeros((1, LANES), F32)
-    for s in range(slab):
-        @pl.when(jnp.logical_not(from_self(s)))
-        def _():
-            remote(fin.at[0], image.at[s], fs.at[0], fr.at[s], dev(s, lax.rem(pos[s] + z, NX), slab * pos[s] + s, core)).wait_recv()
-
-        for p in range(2):
-            r = res[p, s]
-            a = image[s, p] - TV_WEIGHT * smooth[p, s] + TIKHONOV * r
-            out_app[p, s] = a
-            rr, ra, aa = rr + total(r * r), ra + total(r * a), aa + total(a * a)
-
     def exchange(send, recv, ssem, rsem, me, size, where):
         recv[me] = send[...]
 
@@ -448,17 +472,21 @@
         remote(others, others, ssem, rsem, where(lax.rem(me + 1, size))).wait_recv()
         return functools.reduce(jnp.add, [recv[i] for i in range(size)])
 
-    ps1_s[...] = jnp.zeros_like(ps1_s)
-    ps1_s[0:1, :] = rr
-    ps1_s[1:2, :] = ra
-    ps1_s[2:3, :] = aa
     ps2_s[...] = exchange(ps1_s, ps1, p1s, p1r, y, n, at_y)
     sums = jnp.sum(exchange(ps2_s, ps2, p2s, p2r, w, m, at_z), axis=1, keepdims=True)
     norm_old, curvature, applied2 = sums[0:1], sums[1:2], sums[2:3]
     alpha = norm_old / curvature
     norm_new = jnp.maximum(alpha * alpha * applied2 - norm_old, 0.0)
-    out_scal[0:1, :] = jnp.broadcast_to(alpha, (1, cols))
-    out_scal[1:2, :] = jnp.broadcast_to(norm_new / norm_old, (1, cols))
+    out_alpha[...] = jnp.broadcast_to(alpha, (1, cols))
+    out_beta[...] = jnp.broadcast_to(norm_new / norm_old, (1, cols))
+
+    for s in range(slab):
+        @pl.when(jnp.logical_not(from_self(s)))
+        def _():
+            remote(fin.at[0], image.at[s], fs.at[0], fr.at[s], dev(s, lax.rem(pos[s] + z, NX), slab * pos[s] + s, core)).wait_recv()
+
+        for p in range(2):
+            out_app[p, s] = image[s, p]
 
     for recv, ssem, rsem, size, there in ((ps1, p1s, p1r, n, at_y(up_y)), (ps2, p2s, p2r, m, at_z(up_z))):
         others = recv.at[pl.ds(0, size - 1)]
@@ -470,6 +498,10 @@
         def _():
             res_over(j).wait_send()
 
+        @pl.when(jnp.logical_not(from_self(j)))
+        def _():
+            local_over(j).wait_send()
+
         for step in steps:
             maps_over(j, step).wait_send()
 
@@ -514,7 +546,8 @@
     c, s = np.cos(angle), np.sin(angle)
     g = np.block([[c, s], [-s, c]])
     blocks = length // rows
-    g = g.reshape(2, blocks, rows, 2 * length).transpose(1, 0, 2, 3).reshape(2 * length, 2 * length)
+    order = np.arange(2 * length).reshape(2, blocks, rows).transpose(1, 0, 2).reshape(-1)
+    g = g[order][:, order]
     g = g.astype(np.float32)
     h = g.astype(ml_dtypes.bfloat16)
     return np.stack([h, (g - h.astype(np.float32)).astype(ml_dtypes.bfloat16)])
@@ -536,30 +569,30 @@
     def bf16(*shape):
         return pltpu.VMEM(shape, BF16)
 
-    applied, scal = pl.pallas_call(
+    applied, alpha, beta = pl.pallas_call(
         functools.partial(kernel, n, m),
-        out_shape=(jax.ShapeDtypeStruct(solution.shape, F32), jax.ShapeDtypeStruct((2, cols), F32)),
+        out_shape=(jax.ShapeDtypeStruct(solution.shape, F32),) + 2 * (jax.ShapeDtypeStruct((1, cols), F32),),
         in_specs=[vmem, vmem, vmem, hbm, hbm],
-        out_specs=(vmem, vmem),
+        out_specs=(vmem, vmem, vmem),
         scratch_shapes=[
             f32(coils, slab, *chunk), f32(slab, 2 * NX, *chunk), f32(n, *chunk), f32(slab, *chunk), f32(n, *chunk),
-            bf16(2, full, cols), bf16(2, full, cols), bf16(2, full, cols), bf16(2, full, cols),
+            bf16(2 * LANES, cols), bf16(2 * LANES, cols), f32(2 * full, cols), bf16(2 * full, cols), bf16(2 * full, cols),
             pltpu.VMEM(sampling.shape, sampling.dtype), bf16(*g.shape),
             f32(n, *chunk), f32(n // 2, *chunk), f32(n // 2, *chunk), f32(n // 2 // NX, NX, *chunk), f32(2, *chunk),
-            f32(slab, *chunk), f32(*solution.shape),
+            f32(slab, *chunk), f32(*solution.shape), f32(slab, *chunk), f32(n // 2 // NX, *chunk),
             f32(2, *chunk), f32(8, cols), f32(8, cols), f32(*chunk), f32(*chunk), f32(8, cols), f32(8, cols),
             f32(8, LANES), f32(n, 8, LANES), f32(8, LANES), f32(m, 8, LANES),
             dma((2,)), dma((2 * NX * slab,)), dma((2 * NX * slab,)), dma((2 * NX * slab,)), dma((n,)), dma((slab,)), dma((slab,)),
             dma((slab,)), dma((n,)), dma((n // 2 // NX * NX,)), dma((n // 2,)),
             dma((n // 2,)), dma((n // 2,)), dma((n // 2,)), dma((n // 2,)), dma((n // 2 // NX,)), dma((slab,)),
-            dma((5,)), dma((5,)), dma, dma, dma, dma,
+            dma((5,)), dma((5,)), dma((slab,)), dma((n // 2 // NX,)), dma, dma, dma, dma,
         ],
         compiler_params=pltpu.CompilerParams(
             collective_id=0, has_side_effects=True, vmem_limit_bytes=56 * 1024 * 1024
         ),
         name="iteration",
     )(solution, residual, sensitivity, sampling, g)
-    alpha, beta = scal[0], scal[1]
+    alpha, beta = alpha[0], beta[0]
     new_residual = residual - alpha * applied
     return solution + alpha * residual, new_residual, new_residual + beta * residual
 

time: 133 us -> 119 us (0.89)
  Pallas kernels: 130 us -> 117 us
    pallas_call x1, Pallas kernels: 130 us -> 117 us  [body(): pl.pallas_call(functools.partial(kernel, n, m), out_shape=(jax.ShapeDtype...]
where the time goes in v2:
time: 119 us
  Pallas kernels  117 us (98%)
  other arithmetic  1.92 us (2%)
    pallas_call x1, Pallas kernels, body(): pl.pallas_call(functools.partial(kernel, n, m), out_shape=(jax.ShapeDtype...  117 us

profile of v2, /device:TPU:1, one launch (start us, length us, event | category | flops | bytes accessed | tf_op | source)
XLA Modules:
  0.0 119.2 jit_solution(12098811867503394591)
XLA Ops:
  0.6 0.0 copy-start
  0.6 0.0 copy-start.1
  0.7 116.6 %iteration.1 = (f32[2,2,32,512]{3,2,1,0:T(8,128)}, f32[1,512]{1,0:T(1,128)}, f32[1,512]{1,0:T(1,128)}) custom-call(f32[2,2,32,512]{3,2,1,0:T(8,128)} %sol.1, f32[2,2,32,512]{3,2,1,0:T(8,128)} %res.1, bf16[2,8,2,32,512]{4,3,2,1,0:T(8,128)(2,1)} %sens.1, s32[512,512]{1,0:T(8,128)} %samp_in.1, bf16[2,1024,1024]{2,1,0:T(8,128)(2,1)} %constant.2.clone.g_in), custom_call_target="tpu_custom_call" | custom-call | tf_op jit(solution)/shard_map/iteration/pallas_call | solution.py:572
  117.3 0.0 copy-done
  117.3 0.0 copy-done.1
  117.3 1.9 %multiply_add_fusion = (f32[2,2,32,512]{3,2,1,0:T(8,128)}, f32[2,2,32,512]{3,2,1,0:T(8,128)}, f32[2,2,32,512]{3,2,1,0:T(8,128)}) fusion(f32[2,2,32,512]{3,2,1,0:T(8,128)S(1)} %copy-done, f32[512]{0:T(512)} %bitcast.3, f32[2,2,32,512]{3,2,1,0:T(8,128)} %get-tuple-element.7, f32[512]{0:T(512)} %bitcast.2, f32[2,2,32,512]{3,2,1,0:T(8,128)S(1)} %copy-done.1), kind=kLoop, calls=%fused_computation | loop fusion | flops 393216 | bytes 1576960 | tf_op jit(solution)/shard_map/add | solution.py:597
Async XLA Ops:
  0.6 116.6 %copy-start = (f32[2,2,32,512]{3,2,1,0:T(8,128)S(1)}, f32[2,2,32,512]{3,2,1,0:T(8,128)}, u32[]{:S(2)}) copy-start(f32[2,2,32,512]{3,2,1,0:T(8,128)} %res.1) | copy-start | bytes 786436
  0.6 116.6 %copy-start.1 = (f32[2,2,32,512]{3,2,1,0:T(8,128)S(1)}, f32[2,2,32,512]{3,2,1,0:T(8,128)}, u32[]{:S(2)}) copy-start(f32[2,2,32,512]{3,2,1,0:T(8,128)} %sol.1) | copy-start | bytes 786436

commit v3 on v2

--- a/solution.py
+++ b/solution.py
@@ -84,8 +84,8 @@
     def at_z(t):
         return (y, t)
 
-    def across(p, k):
-        return (p, p + 1 - 2 * lax.rem(p, 2), lax.rem(p + 2, NX), NX - 1 - p)[k]
+    def xor(a, b):
+        return 2 * lax.rem(a // 2 + b // 2, 2) + lax.rem(a + b, 2)
 
     def remote(src, dst, ssem, rsem, device):
         return pltpu.make_async_remote_copy(
@@ -108,10 +108,10 @@
     loop(1, m, lambda k: hail(at_z(lax.rem(w + k, m))))
     for j in range(slab):
         loop(1, NX, lambda k: hail(dev(j, lax.rem(pos[j] + k, NX), z, sib)))
-        hail(dev(j, lax.rem(pos[j] + z, NX), slab * pos[j] + j, core))
+        hail(dev(j, xor(pos[j], sp), slab * pos[j] + j, core))
 
     def from_self(j):
-        return jnp.logical_and(lax.rem(z, NX) == 0, slab * pos[j] + j == z)
+        return jnp.logical_and(sp == 0, slab * pos[j] + j == z)
 
     loads = [
         pltpu.make_async_copy(a, b, csem.at[i]) for i, (a, b) in enumerate([(g_in, g), (samp_in, samp)])
@@ -136,10 +136,10 @@
 
     pl.semaphore_wait(barrier, n + m - 2 + slab * NX)
 
-    moved = lax.rem(z, NX) != 0
+    moved = sp != 0
 
     def res_over(j):
-        return remote(res.at[:, j], xrel.at[j], xrs.at[j], xrr.at[j], dev(j, lax.rem(pos[j] + z, NX), z, core))
+        return remote(res.at[:, j], xrel.at[j], xrs.at[j], xrr.at[j], dev(j, xor(pos[j], sp), z, core))
 
     for j in range(slab):
         @pl.when(moved)
@@ -150,12 +150,15 @@
         def _():
             xrel[j] = res[:, j]
 
-    steps = [(0, 1), (1, 0), (3, 0), (1, 1), (3, 1), (2, 0), (2, 1)]
+    steps = [(k, c) for k in range(NX) for c in range(2)]
 
     def partner(j, step):
-        p = across(pos[j], step[0])
+        p = xor(pos[j], xor(sp, step[0]))
         c = sib if step[1] else core
         return p, c, 2 * p + c
+
+    def hops(step):
+        return jnp.logical_or(sp != step[0], step[1] > 0)
 
     def maps_over(j, step):
         p, c, t = partner(j, step)
@@ -164,7 +167,9 @@
 
     for step in steps:
         for j in range(slab):
-            maps_over(j, step).start()
+            @pl.when(hops(step))
+            def _():
+                maps_over(j, step).start()
 
     halo1 = [
         remote(sol.at[:, 0], hz.at[0], hs.at[0], hr.at[0], at_z(down_z)),
@@ -191,12 +196,8 @@
         def _():
             srecv[slot] = src[...]
 
-    for j in range(slab):
-        t = 2 * pos[j] + core
-        forward_maps(sbuf.at[t, j], j, t)
-
     def forward_res(j):
-        zt = slab * lax.rem(pos[j] + NX - lax.rem(z, NX), NX) + j
+        zt = slab * xor(pos[j], sp) + j
         return zt, remote(xrel.at[j], xall.at[y], xzs.at[j], xar.at[y], dev(0, x, zt, core))
 
     for j in range(slab):
@@ -216,17 +217,24 @@
 
     def relay_maps(step):
         for j in range(slab):
-            _, _, t = partner(j, step)
-            remote(sbuf.at[t, j], relay.at[j, t], xls.at[line * j + t], xlr.at[line * j + t], dev(j, pos[j], z, sib)).wait_recv()
-            forward_maps(relay.at[j, t], j, t)
+            p, c, t = partner(j, step)
+
+            @pl.when(hops(step))
+            def _():
+                remote(sbuf.at[t, j], relay.at[j, t], xls.at[line * j + t], xlr.at[line * j + t], dev(j, p, z, c)).wait_recv()
+                forward_maps(relay.at[j, t], j, t)
+
+            @pl.when(jnp.logical_not(hops(step)))
+            def _():
+                forward_maps(sbuf.at[t, j], j, t)
 
     for step in steps:
         relay_maps(step)
 
-    first = lax.rem(lp + NX - lax.rem(sp, NX), NX)
+    first = 2 * xor(lp, sp)
 
     def hand(slot, i, k):
-        p = lax.rem(lp + k, NX)
+        p = xor(lp, k)
         return remote(xall.at[slot], xall.at[slot], ms.at[i * NX + k], xar.at[slot], on_line(p, z, core))
 
     def to_other(zz):
@@ -234,7 +242,7 @@
         return remote(xall.at[slot], xall.at[slot], os.at[zz], xar.at[slot], on_line(lp, z, sib))
 
     for i in range(nz // NX):
-        zz = first + NX * i
+        zz = first + i
         slot = 2 * zz + core
 
         @pl.when(zz != z)
@@ -291,9 +299,9 @@
 
     for k in range(1, NX):
         for i in range(nz // NX):
-            zz = lax.rem(first + k, NX) + NX * i
+            zz = 2 * xor(xor(lp, k), sp) + i
             slot = 2 * zz + core
-            remote(xall.at[slot], xall.at[slot], ms.at[0], xar.at[slot], on_line(lax.rem(lp + k, NX), z, core)).wait_recv()
+            remote(xall.at[slot], xall.at[slot], ms.at[0], xar.at[slot], on_line(xor(lp, k), z, core)).wait_recv()
             to_other(zz).start()
 
     per = 4
@@ -315,8 +323,8 @@
     at_top = jnp.logical_and(row == 0, y > 0)
 
     def local_over(j):
-        there = dev(j, lax.rem(pos[j] + z, NX), slab * pos[j] + j, core)
-        return remote(local.at[j], local_in.at[z // NX], ls.at[j], lr.at[z // NX], there)
+        there = dev(j, xor(pos[j], sp), slab * pos[j] + j, core)
+        return remote(local.at[j], local_in.at[odd], ls.at[j], lr.at[odd], there)
 
     def send_local():
         for h in halo2:
@@ -335,7 +343,7 @@
 
             @pl.when(from_self(j))
             def _():
-                local_in[z // NX] = local[j]
+                local_in[odd] = local[j]
 
     full = n * rows
     scale = 1.0 / (full * cols)
@@ -344,7 +352,7 @@
     loads[1].wait()
 
     def forward(i):
-        q = lax.rem(y // per + groups - 1 - i, groups)
+        q = xor(xor(lp, sp), i)
         last = i == groups - 1
 
         @pl.when(last)
@@ -385,8 +393,9 @@
         return remote(part.at[2 * zz + sib], pair.at[zz], prs.at[zz], prr.at[zz], on_line(lp, z, sib))
 
     def to_adder(zz):
-        t = lax.rem(sp + zz, NX)
-        return t, remote(tot.at[zz], gath.at[zz // NX, lp], gs.at[zz], gr.at[NX * (zz // NX) + lp], on_line(t, z, core))
+        t = xor(sp, zz // 2)
+        i = lax.rem(zz, 2)
+        return t, remote(tot.at[zz], gath.at[i, lp], gs.at[zz], gr.at[NX * i + lp], on_line(t, z, core))
 
     def add_pair(zz):
         to_sib(zz).wait_recv()
@@ -398,14 +407,14 @@
             cp.start()
 
     def home(i):
-        zz = first + NX * i
+        zz = first + i
         return zz, remote(fin.at[i], image.at[odd], fs.at[i], fr.at[odd], on_line(sp, zz, core))
 
     def add_line(i):
         zz, cp = home(i)
         v = tot[zz]
         for k in range(1, NX):
-            t = lax.rem(lp + k, NX)
+            t = xor(lp, k)
             remote(tot.at[zz], gath.at[i, t], gs.at[zz], gr.at[NX * i + t], on_line(t, z, core)).wait_recv()
             v = v + gath[i, t]
 
@@ -430,7 +439,11 @@
             fin[i] = v
             cp.start()
 
-    def inverse(q):
+    def block_at(i):
+        return xor(xor(lp, sp), 2 + i - (i // 2) * (2 * i - 1))
+
+    def inverse(i):
+        q = block_at(i)
         at = pl.ds(pl.multiple_of(2 * q * tile, 2 * tile), 2 * tile)
         v = dot3(g[0, at], g[1, at], yh[...], yl[...])
         ah, al = split(interleave(v[:tile], -v[tile:]))
@@ -445,20 +458,17 @@
         for t in range(per // 2):
             to_sib(q * per // 2 + t).start()
 
-        @pl.when(q > 0)
+        @pl.when(i > 0)
         def _():
             for t in range(per // 2):
-                add_pair((q - 1) * per // 2 + t)
-
-        @pl.when(q == groups - 1)
-        def _():
-            add_line(0)
+                add_pair(block_at(i - 1) * per // 2 + t)
 
     ps1_s[...] = jnp.zeros_like(ps1_s)
     loop(0, groups, inverse)
     for t in range(per // 2):
-        add_pair((groups - 1) * per // 2 + t)
-    add_line(1)
+        add_pair(first + t)
+    for i in range(nz // NX):
+        add_line(i)
 
     def exchange(send, recv, ssem, rsem, me, size, where):
         recv[me] = send[...]
@@ -483,7 +493,7 @@
     for s in range(slab):
         @pl.when(jnp.logical_not(from_self(s)))
         def _():
-            remote(fin.at[0], image.at[s], fs.at[0], fr.at[s], dev(s, lax.rem(pos[s] + z, NX), slab * pos[s] + s, core)).wait_recv()
+            remote(fin.at[0], image.at[s], fs.at[0], fr.at[s], dev(s, xor(pos[s], sp), slab * pos[s] + s, core)).wait_recv()
 
         for p in range(2):
             out_app[p, s] = image[s, p]
@@ -503,7 +513,9 @@
             local_over(j).wait_send()
 
         for step in steps:
-            maps_over(j, step).wait_send()
+            @pl.when(hops(step))
+            def _():
+                maps_over(j, step).wait_send()
 
         def sent_maps(t):
             zt, _, cp = pass_on(sbuf.at[0, j], j, t)
@@ -521,7 +533,7 @@
 
     for i in range(nz // NX):
         for k in range(1, NX):
-            hand(2 * (first + NX * i) + core, i, k).wait_send()
+            hand(2 * (first + i) + core, i, k).wait_send()
         zz, cp = home(i)
 
         @pl.when(jnp.logical_not(jnp.logical_and(sp == lp, zz == z)))

time: 119 us -> 125 us (1.050); the launches traced: 119 us -> 123 us
  Pallas kernels: 117 us -> 121 us
    pallas_call x1, Pallas kernels: 117 us -> 121 us  [body(): pl.pallas_call(functools.partial(kernel, n, m), out_shape=(jax.ShapeDtype...]
where the time goes in v3:
time: 125 us; the launch traced here: 123 us
  Pallas kernels  121 us (97%)
  other arithmetic  1.92 us (2%)
    pallas_call x1, Pallas kernels, body(): pl.pallas_call(functools.partial(kernel, n, m), out_shape=(jax.ShapeDtype...  121 us

profile of v3, /device:TPU:1, one launch (start us, length us, event | category | flops | bytes accessed | tf_op | source)
XLA Modules:
  0.0 123.1 jit_solution(6673054024328285117)
XLA Ops:
  0.6 0.0 copy-start
  0.6 0.0 copy-start.1
  0.7 120.5 %iteration.1 = (f32[2,2,32,512]{3,2,1,0:T(8,128)}, f32[1,512]{1,0:T(1,128)}, f32[1,512]{1,0:T(1,128)}) custom-call(f32[2,2,32,512]{3,2,1,0:T(8,128)} %sol.1, f32[2,2,32,512]{3,2,1,0:T(8,128)} %res.1, bf16[2,8,2,32,512]{4,3,2,1,0:T(8,128)(2,1)} %sens.1, s32[512,512]{1,0:T(8,128)} %samp_in.1, bf16[2,1024,1024]{2,1,0:T(8,128)(2,1)} %constant.2.clone.g_in), custom_call_target="tpu_custom_call" | custom-call | tf_op jit(solution)/shard_map/iteration/pallas_call | solution.py:584
  121.2 0.0 copy-done
  121.2 0.0 copy-done.1
  121.2 1.9 %multiply_add_fusion = (f32[2,2,32,512]{3,2,1,0:T(8,128)}, f32[2,2,32,512]{3,2,1,0:T(8,128)}, f32[2,2,32,512]{3,2,1,0:T(8,128)}) fusion(f32[2,2,32,512]{3,2,1,0:T(8,128)S(1)} %copy-done, f32[512]{0:T(512)} %bitcast.3, f32[2,2,32,512]{3,2,1,0:T(8,128)} %get-tuple-element.7, f32[512]{0:T(512)} %bitcast.2, f32[2,2,32,512]{3,2,1,0:T(8,128)S(1)} %copy-done.1), kind=kLoop, calls=%fused_computation | loop fusion | flops 393216 | bytes 1576960 | tf_op jit(solution)/shard_map/add | solution.py:609
Async XLA Ops:
  0.6 120.5 %copy-start = (f32[2,2,32,512]{3,2,1,0:T(8,128)S(1)}, f32[2,2,32,512]{3,2,1,0:T(8,128)}, u32[]{:S(2)}) copy-start(f32[2,2,32,512]{3,2,1,0:T(8,128)} %res.1) | copy-start | bytes 786436
  0.6 120.5 %copy-start.1 = (f32[2,2,32,512]{3,2,1,0:T(8,128)S(1)}, f32[2,2,32,512]{3,2,1,0:T(8,128)}, u32[]{:S(2)}) copy-start(f32[2,2,32,512]{3,2,1,0:T(8,128)} %sol.1) | copy-start | bytes 786436

commit v4 on v3

--- a/solution.py
+++ b/solution.py
@@ -84,8 +84,16 @@
     def at_z(t):
         return (y, t)
 
-    def xor(a, b):
-        return 2 * lax.rem(a // 2 + b // 2, 2) + lax.rem(a + b, 2)
+    other = (yy, x)
+
+    def around(t):
+        return lax.rem(t + 4 * NX, NX)
+
+    def shift(j):
+        return sp + other[j] + 2 * j
+
+    def rows_at(k):
+        return around(sp - x - yy - 2 * odd - k)
 
     def remote(src, dst, ssem, rsem, device):
         return pltpu.make_async_remote_copy(
@@ -108,10 +116,10 @@
     loop(1, m, lambda k: hail(at_z(lax.rem(w + k, m))))
     for j in range(slab):
         loop(1, NX, lambda k: hail(dev(j, lax.rem(pos[j] + k, NX), z, sib)))
-        hail(dev(j, xor(pos[j], sp), slab * pos[j] + j, core))
+        hail(dev(j, around(pos[j] - shift(j)), slab * pos[j] + j, core))
 
     def from_self(j):
-        return jnp.logical_and(sp == 0, slab * pos[j] + j == z)
+        return jnp.logical_and(around(shift(j)) == 0, slab * pos[j] + j == z)
 
     loads = [
         pltpu.make_async_copy(a, b, csem.at[i]) for i, (a, b) in enumerate([(g_in, g), (samp_in, samp)])
@@ -136,38 +144,36 @@
 
     pl.semaphore_wait(barrier, n + m - 2 + slab * NX)
 
-    moved = sp != 0
+    def moved(j):
+        return around(shift(j)) != 0
 
     def res_over(j):
-        return remote(res.at[:, j], xrel.at[j], xrs.at[j], xrr.at[j], dev(j, xor(pos[j], sp), z, core))
+        return remote(res.at[:, j], xrel.at[j], xrs.at[j], xrr.at[j], dev(j, around(pos[j] - shift(j)), z, core))
 
     for j in range(slab):
-        @pl.when(moved)
+        @pl.when(moved(j))
         def _():
             res_over(j).start()
 
-        @pl.when(jnp.logical_not(moved))
+        @pl.when(jnp.logical_not(moved(j)))
         def _():
             xrel[j] = res[:, j]
 
     steps = [(k, c) for k in range(NX) for c in range(2)]
 
-    def partner(j, step):
-        p = xor(pos[j], xor(sp, step[0]))
+    def hops(j, step):
+        return jnp.logical_or(around(shift(j) + step[0]) != 0, step[1] > 0)
+
+    def maps_over(j, step):
+        p = around(pos[j] - shift(j) - step[0])
         c = sib if step[1] else core
-        return p, c, 2 * p + c
-
-    def hops(step):
-        return jnp.logical_or(sp != step[0], step[1] > 0)
-
-    def maps_over(j, step):
-        p, c, t = partner(j, step)
+        t = 2 * p + c
         me = 2 * pos[j] + core
         return remote(sbuf.at[t, j], relay.at[j, me], xls.at[line * j + t], xlr.at[line * j + me], dev(j, p, z, c))
 
     for step in steps:
         for j in range(slab):
-            @pl.when(hops(step))
+            @pl.when(hops(j, step))
             def _():
                 maps_over(j, step).start()
 
@@ -197,11 +203,11 @@
             srecv[slot] = src[...]
 
     def forward_res(j):
-        zt = slab * xor(pos[j], sp) + j
+        zt = slab * around(pos[j] + shift(j)) + j
         return zt, remote(xrel.at[j], xall.at[y], xzs.at[j], xar.at[y], dev(0, x, zt, core))
 
     for j in range(slab):
-        @pl.when(moved)
+        @pl.when(moved(j))
         def _():
             res_over(j).wait_recv()
 
@@ -217,24 +223,26 @@
 
     def relay_maps(step):
         for j in range(slab):
-            p, c, t = partner(j, step)
-
-            @pl.when(hops(step))
+            p = around(pos[j] + shift(j) + step[0])
+            c = sib if step[1] else core
+            t = 2 * p + c
+
+            @pl.when(hops(j, step))
             def _():
                 remote(sbuf.at[t, j], relay.at[j, t], xls.at[line * j + t], xlr.at[line * j + t], dev(j, p, z, c)).wait_recv()
                 forward_maps(relay.at[j, t], j, t)
 
-            @pl.when(jnp.logical_not(hops(step)))
+            @pl.when(jnp.logical_not(hops(j, step)))
             def _():
                 forward_maps(sbuf.at[t, j], j, t)
 
     for step in steps:
         relay_maps(step)
 
-    first = 2 * xor(lp, sp)
+    first = 2 * rows_at(0)
 
     def hand(slot, i, k):
-        p = xor(lp, k)
+        p = around(lp + k)
         return remote(xall.at[slot], xall.at[slot], ms.at[i * NX + k], xar.at[slot], on_line(p, z, core))
 
     def to_other(zz):
@@ -299,9 +307,9 @@
 
     for k in range(1, NX):
         for i in range(nz // NX):
-            zz = 2 * xor(xor(lp, k), sp) + i
+            zz = 2 * rows_at(k) + i
             slot = 2 * zz + core
-            remote(xall.at[slot], xall.at[slot], ms.at[0], xar.at[slot], on_line(xor(lp, k), z, core)).wait_recv()
+            remote(xall.at[slot], xall.at[slot], ms.at[0], xar.at[slot], on_line(around(lp + k), z, core)).wait_recv()
             to_other(zz).start()
 
     per = 4
@@ -323,7 +331,7 @@
     at_top = jnp.logical_and(row == 0, y > 0)
 
     def local_over(j):
-        there = dev(j, xor(pos[j], sp), slab * pos[j] + j, core)
+        there = dev(j, around(pos[j] - shift(j)), slab * pos[j] + j, core)
         return remote(local.at[j], local_in.at[odd], ls.at[j], lr.at[odd], there)
 
     def send_local():
@@ -352,7 +360,7 @@
     loads[1].wait()
 
     def forward(i):
-        q = xor(xor(lp, sp), i)
+        q = rows_at(i)
         last = i == groups - 1
 
         @pl.when(last)
@@ -393,7 +401,7 @@
         return remote(part.at[2 * zz + sib], pair.at[zz], prs.at[zz], prr.at[zz], on_line(lp, z, sib))
 
     def to_adder(zz):
-        t = xor(sp, zz // 2)
+        t = around(lp + rows_at(0) - zz // 2)
         i = lax.rem(zz, 2)
         return t, remote(tot.at[zz], gath.at[i, lp], gs.at[zz], gr.at[NX * i + lp], on_line(t, z, core))
 
@@ -414,7 +422,7 @@
         zz, cp = home(i)
         v = tot[zz]
         for k in range(1, NX):
-            t = xor(lp, k)
+            t = around(lp + k)
             remote(tot.at[zz], gath.at[i, t], gs.at[zz], gr.at[NX * i + t], on_line(t, z, core)).wait_recv()
             v = v + gath[i, t]
 
@@ -440,7 +448,7 @@
             cp.start()
 
     def block_at(i):
-        return xor(xor(lp, sp), 2 + i - (i // 2) * (2 * i - 1))
+        return rows_at(2 + i - (i // 2) * (2 * i - 1))
 
     def inverse(i):
         q = block_at(i)
@@ -493,7 +501,7 @@
     for s in range(slab):
         @pl.when(jnp.logical_not(from_self(s)))
         def _():
-            remote(fin.at[0], image.at[s], fs.at[0], fr.at[s], dev(s, xor(pos[s], sp), slab * pos[s] + s, core)).wait_recv()
+            remote(fin.at[0], image.at[s], fs.at[0], fr.at[s], dev(s, around(pos[s] - shift(s)), slab * pos[s] + s, core)).wait_recv()
 
         for p in range(2):
             out_app[p, s] = image[s, p]
@@ -504,7 +512,7 @@
     for h in halo1 + halo2:
         h.wait_send()
     for j in range(slab):
-        @pl.when(moved)
+        @pl.when(moved(j))
         def _():
             res_over(j).wait_send()
 
@@ -513,7 +521,7 @@
             local_over(j).wait_send()
 
         for step in steps:
-            @pl.when(hops(step))
+            @pl.when(hops(j, step))
             def _():
                 maps_over(j, step).wait_send()
 

time: 125 us -> 120 us (0.960); the launches traced: 123 us -> 120 us
  Pallas kernels: 121 us -> 117 us
    pallas_call x1, Pallas kernels: 121 us -> 117 us  [body(): pl.pallas_call(functools.partial(kernel, n, m), out_shape=(jax.ShapeDtype...]
where the time goes in v4:
time: 120 us
  Pallas kernels  117 us (98%)
  other arithmetic  1.92 us (2%)
    pallas_call x1, Pallas kernels, body(): pl.pallas_call(functools.partial(kernel, n, m), out_shape=(jax.ShapeDtype...  117 us

profile of v4, /device:TPU:1, one launch (start us, length us, event | category | flops | bytes accessed | tf_op | source)
XLA Modules:
  0.0 119.8 jit_solution(14987580431339632754)
XLA Ops:
  0.6 0.0 copy-start
  0.6 0.0 copy-start.1
  0.7 117.2 %iteration.1 = (f32[2,2,32,512]{3,2,1,0:T(8,128)}, f32[1,512]{1,0:T(1,128)}, f32[1,512]{1,0:T(1,128)}) custom-call(f32[2,2,32,512]{3,2,1,0:T(8,128)} %sol.1, f32[2,2,32,512]{3,2,1,0:T(8,128)} %res.1, bf16[2,8,2,32,512]{4,3,2,1,0:T(8,128)(2,1)} %sens.1, s32[512,512]{1,0:T(8,128)} %samp_in.1, bf16[2,1024,1024]{2,1,0:T(8,128)(2,1)} %constant.2.clone.g_in), custom_call_target="tpu_custom_call" | custom-call | tf_op jit(solution)/shard_map/iteration/pallas_call | solution.py:592
  117.8 0.0 copy-done
  117.9 0.0 copy-done.1
  117.9 1.9 %multiply_add_fusion = (f32[2,2,32,512]{3,2,1,0:T(8,128)}, f32[2,2,32,512]{3,2,1,0:T(8,128)}, f32[2,2,32,512]{3,2,1,0:T(8,128)}) fusion(f32[2,2,32,512]{3,2,1,0:T(8,128)S(1)} %copy-done, f32[512]{0:T(512)} %bitcast.3, f32[2,2,32,512]{3,2,1,0:T(8,128)} %get-tuple-element.7, f32[512]{0:T(512)} %bitcast.2, f32[2,2,32,512]{3,2,1,0:T(8,128)S(1)} %copy-done.1), kind=kLoop, calls=%fused_computation | loop fusion | flops 393216 | bytes 1576960 | tf_op jit(solution)/shard_map/add | solution.py:617
Async XLA Ops:
  0.6 117.2 %copy-start = (f32[2,2,32,512]{3,2,1,0:T(8,128)S(1)}, f32[2,2,32,512]{3,2,1,0:T(8,128)}, u32[]{:S(2)}) copy-start(f32[2,2,32,512]{3,2,1,0:T(8,128)} %res.1) | copy-start | bytes 786436
  0.6 117.2 %copy-start.1 = (f32[2,2,32,512]{3,2,1,0:T(8,128)S(1)}, f32[2,2,32,512]{3,2,1,0:T(8,128)}, u32[]{:S(2)}) copy-start(f32[2,2,32,512]{3,2,1,0:T(8,128)} %sol.1) | copy-start | bytes 786436

commit v5 on v4

--- a/solution.py
+++ b/solution.py
@@ -50,9 +50,9 @@
 
 
 def kernel(
-    n, m, sol, res, sens, samp_in, g_in,
+    n, m, sol_in, res_in, sens_in, samp_in, g_in,
     out_app, out_alpha, out_beta,
-    sbuf, relay, srecv, xrel, xall, vh, vl, yacc, yh, yl, samp, g,
+    sol, res, sens, sbuf, relay, srecv, xrel, xall, vh, vl, yacc, yh, yl, samp, g,
     part, pair, tot, gath, fin, image, smooth, local, local_in,
     hz, hy_s, hy, qz_s, qz, qy_s, qy, ps1_s, ps1, ps2_s, ps2,
     csem, xls, xlr, zs, zr, xrs, xrr, xzs, xar, ms, os,
@@ -107,6 +107,13 @@
 
         lax.fori_loop(lo, hi, step, 0)
 
+    loads = [
+        pltpu.make_async_copy(a, b, csem.at[i])
+        for i, (a, b) in enumerate([(sens_in, sens), (res_in, res), (sol_in, sol), (g_in, g), (samp_in, samp)])
+    ]
+    for c in loads:
+        c.start()
+
     barrier = pltpu.get_barrier_semaphore()
 
     def hail(device):
@@ -121,18 +128,15 @@
     def from_self(j):
         return jnp.logical_and(around(shift(j)) == 0, slab * pos[j] + j == z)
 
-    loads = [
-        pltpu.make_async_copy(a, b, csem.at[i]) for i, (a, b) in enumerate([(g_in, g), (samp_in, samp)])
-    ]
-    for c in loads:
-        c.start()
-
     def widen(c):
         for j in range(slab):
             sbuf[c, j, 0] = sens[0, c, j].astype(F32)
             sbuf[c, j, 1] = sens[1, c, j].astype(F32)
 
+    loads[0].wait()
     loop(0, line, widen)
+    loads[1].wait()
+    loads[2].wait()
 
     up_y, down_y = lax.rem(y + 1, n), lax.rem(y + n - 1, n)
     up_z, down_z = lax.rem(w + 1, m), lax.rem(w + m - 1, m)
@@ -144,38 +148,58 @@
 
     pl.semaphore_wait(barrier, n + m - 2 + slab * NX)
 
-    def moved(j):
-        return around(shift(j)) != 0
-
-    def res_over(j):
-        return remote(res.at[:, j], xrel.at[j], xrs.at[j], xrr.at[j], dev(j, around(pos[j] - shift(j)), z, core))
-
-    for j in range(slab):
-        @pl.when(moved(j))
-        def _():
-            res_over(j).start()
-
-        @pl.when(jnp.logical_not(moved(j)))
-        def _():
-            xrel[j] = res[:, j]
-
-    steps = [(k, c) for k in range(NX) for c in range(2)]
-
-    def hops(j, step):
-        return jnp.logical_or(around(shift(j) + step[0]) != 0, step[1] > 0)
-
-    def maps_over(j, step):
-        p = around(pos[j] - shift(j) - step[0])
-        c = sib if step[1] else core
+    def pass_on(src, j, t):
+        zt = slab * (t // 2) + j
+        slot = 2 * z + lax.rem(t, 2)
+        cp = remote(src, srecv.at[slot], zs.at[line * j + t], zr.at[slot], dev(0, x, zt, core))
+        return zt, slot, cp
+
+    def forward_maps(src, j, t):
+        zt, slot, cp = pass_on(src, j, t)
+
+        @pl.when(zt != z)
+        def _():
+            cp.start()
+
+        @pl.when(zt == z)
+        def _():
+            srecv[slot] = src[...]
+
+    def maps_over(j, p, c):
         t = 2 * p + c
         me = 2 * pos[j] + core
         return remote(sbuf.at[t, j], relay.at[j, me], xls.at[line * j + t], xlr.at[line * j + me], dev(j, p, z, c))
 
-    for step in steps:
+    for j in range(slab):
+        t = 2 * pos[j] + core
+        forward_maps(sbuf.at[t, j], j, t)
+        maps_over(j, pos[j], sib).start()
+
+    def moved(j):
+        return around(shift(j)) != 0
+
+    def res_over(j):
+        return remote(res.at[:, j], xrel.at[j], xrs.at[j], xrr.at[j], dev(j, around(pos[j] - shift(j)), z, core))
+
+    for j in range(slab):
+        @pl.when(moved(j))
+        def _():
+            res_over(j).start()
+
+        @pl.when(jnp.logical_not(moved(j)))
+        def _():
+            xrel[j] = res[:, j]
+
+    steps = [(k, c) for k in range(NX) for c in (core, sib)]
+
+    def hops(j, k):
+        return around(shift(j) + k) != 0
+
+    for k, c in steps:
         for j in range(slab):
-            @pl.when(hops(j, step))
-            def _():
-                maps_over(j, step).start()
+            @pl.when(hops(j, k))
+            def _():
+                maps_over(j, around(pos[j] - shift(j) - k), c).start()
 
     halo1 = [
         remote(sol.at[:, 0], hz.at[0], hs.at[0], hr.at[0], at_z(down_z)),
@@ -185,22 +209,13 @@
     for h in halo1:
         h.start()
 
-    def pass_on(src, j, t):
-        zt = slab * (t // 2) + j
-        slot = 2 * z + lax.rem(t, 2)
-        cp = remote(src, srecv.at[slot], zs.at[line * j + t], zr.at[slot], dev(0, x, zt, core))
-        return zt, slot, cp
-
-    def forward_maps(src, j, t):
-        zt, slot, cp = pass_on(src, j, t)
-
-        @pl.when(zt != z)
-        def _():
-            cp.start()
-
-        @pl.when(zt == z)
-        def _():
-            srecv[slot] = src[...]
+    def relay_maps(j, p, c):
+        t = 2 * p + c
+        remote(sbuf.at[t, j], relay.at[j, t], xls.at[line * j + t], xlr.at[line * j + t], dev(j, p, z, c)).wait_recv()
+        forward_maps(relay.at[j, t], j, t)
+
+    for j in range(slab):
+        relay_maps(j, pos[j], sib)
 
     def forward_res(j):
         zt = slab * around(pos[j] + shift(j)) + j
@@ -221,23 +236,11 @@
         def _():
             xall[y] = xrel[j]
 
-    def relay_maps(step):
+    for k, c in steps:
         for j in range(slab):
-            p = around(pos[j] + shift(j) + step[0])
-            c = sib if step[1] else core
-            t = 2 * p + c
-
-            @pl.when(hops(j, step))
-            def _():
-                remote(sbuf.at[t, j], relay.at[j, t], xls.at[line * j + t], xlr.at[line * j + t], dev(j, p, z, c)).wait_recv()
-                forward_maps(relay.at[j, t], j, t)
-
-            @pl.when(jnp.logical_not(hops(j, step)))
-            def _():
-                forward_maps(sbuf.at[t, j], j, t)
-
-    for step in steps:
-        relay_maps(step)
+            @pl.when(hops(j, k))
+            def _():
+                relay_maps(j, around(pos[j] + shift(j) + k), c)
 
     first = 2 * rows_at(0)
 
@@ -356,8 +359,8 @@
     full = n * rows
     scale = 1.0 / (full * cols)
     yacc[...] = jnp.zeros_like(yacc)
-    loads[0].wait()
-    loads[1].wait()
+    loads[3].wait()
+    loads[4].wait()
 
     def forward(i):
         q = rows_at(i)
@@ -520,10 +523,11 @@
         def _():
             local_over(j).wait_send()
 
-        for step in steps:
-            @pl.when(hops(j, step))
-            def _():
-                maps_over(j, step).wait_send()
+        maps_over(j, pos[j], sib).wait_send()
+        for k, c in steps:
+            @pl.when(hops(j, k))
+            def _():
+                maps_over(j, around(pos[j] - shift(j) - k), c).wait_send()
 
         def sent_maps(t):
             zt, _, cp = pass_on(sbuf.at[0, j], j, t)
@@ -592,9 +596,10 @@
     applied, alpha, beta = pl.pallas_call(
         functools.partial(kernel, n, m),
         out_shape=(jax.ShapeDtypeStruct(solution.shape, F32),) + 2 * (jax.ShapeDtypeStruct((1, cols), F32),),
-        in_specs=[vmem, vmem, vmem, hbm, hbm],
+        in_specs=5 * [hbm],
         out_specs=(vmem, vmem, vmem),
         scratch_shapes=[
+            f32(*solution.shape), f32(*residual.shape), bf16(*sensitivity.shape),
             f32(coils, slab, *chunk), f32(slab, 2 * NX, *chunk), f32(n, *chunk), f32(slab, *chunk), f32(n, *chunk),
             bf16(2 * LANES, cols), bf16(2 * LANES, cols), f32(2 * full, cols), bf16(2 * full, cols), bf16(2 * full, cols),
             pltpu.VMEM(sampling.shape, sampling.dtype), bf16(*g.shape),
@@ -602,7 +607,7 @@
             f32(slab, *chunk), f32(*solution.shape), f32(slab, *chunk), f32(n // 2 // NX, *chunk),
             f32(2, *chunk), f32(8, cols), f32(8, cols), f32(*chunk), f32(*chunk), f32(8, cols), f32(8, cols),
             f32(8, LANES), f32(n, 8, LANES), f32(8, LANES), f32(m, 8, LANES),
-            dma((2,)), dma((2 * NX * slab,)), dma((2 * NX * slab,)), dma((2 * NX * slab,)), dma((n,)), dma((slab,)), dma((slab,)),
+            dma((5,)), dma((2 * NX * slab,)), dma((2 * NX * slab,)), dma((2 * NX * slab,)), dma((n,)), dma((slab,)), dma((slab,)),
             dma((slab,)), dma((n,)), dma((n // 2 // NX * NX,)), dma((n // 2,)),
             dma((n // 2,)), dma((n // 2,)), dma((n // 2,)), dma((n // 2,)), dma((n // 2 // NX,)), dma((slab,)),
             dma((5,)), dma((5,)), dma((slab,)), dma((n // 2 // NX,)), dma, dma, dma, dma,

time: 120 us -> 120 us (level)
  no operation moved by 1% of the time
where the time goes in v5:
time: 120 us
  Pallas kernels  117 us (98%)
  other arithmetic  1.92 us (2%)
    pallas_call x1, Pallas kernels, body(): pl.pallas_call(functools.partial(kernel, n, m), out_shape=(jax.ShapeDtype...  117 us

profile of v5, /device:TPU:1, one launch (start us, length us, event | category | flops | bytes accessed | tf_op | source)
XLA Modules:
  0.0 119.6 jit_solution(1885792699300088238)
XLA Ops:
  0.6 0.0 copy-start
  0.6 0.0 copy-start.1
  0.7 117.0 %iteration.1 = (f32[2,2,32,512]{3,2,1,0:T(8,128)}, f32[1,512]{1,0:T(1,128)}, f32[1,512]{1,0:T(1,128)}) custom-call(f32[2,2,32,512]{3,2,1,0:T(8,128)} %sol_in.1, f32[2,2,32,512]{3,2,1,0:T(8,128)} %res_in.1, bf16[2,8,2,32,512]{4,3,2,1,0:T(8,128)(2,1)} %sens_in.1, s32[512,512]{1,0:T(8,128)} %samp_in.1, bf16[2,1024,1024]{2,1,0:T(8,128)(2,1)} %constant.2.clone.g_in), custom_call_target="tpu_custom_call" | custom-call | tf_op jit(solution)/shard_map/iteration/pallas_call | solution.py:596
  117.7 0.0 copy-done
  117.7 0.0 copy-done.1
  117.7 1.9 %multiply_add_fusion = (f32[2,2,32,512]{3,2,1,0:T(8,128)}, f32[2,2,32,512]{3,2,1,0:T(8,128)}, f32[2,2,32,512]{3,2,1,0:T(8,128)}) fusion(f32[2,2,32,512]{3,2,1,0:T(8,128)S(1)} %copy-done, f32[512]{0:T(512)} %bitcast.3, f32[2,2,32,512]{3,2,1,0:T(8,128)} %get-tuple-element.7, f32[512]{0:T(512)} %bitcast.2, f32[2,2,32,512]{3,2,1,0:T(8,128)S(1)} %copy-done.1), kind=kLoop, calls=%fused_computation | loop fusion | flops 393216 | bytes 1576960 | tf_op jit(solution)/shard_map/add | solution.py:622
Async XLA Ops:
  0.6 117.0 %copy-start = (f32[2,2,32,512]{3,2,1,0:T(8,128)S(1)}, f32[2,2,32,512]{3,2,1,0:T(8,128)}, u32[]{:S(2)}) copy-start(f32[2,2,32,512]{3,2,1,0:T(8,128)} %res_in.1) | copy-start | bytes 786436
  0.6 117.0 %copy-start.1 = (f32[2,2,32,512]{3,2,1,0:T(8,128)S(1)}, f32[2,2,32,512]{3,2,1,0:T(8,128)}, u32[]{:S(2)}) copy-start(f32[2,2,32,512]{3,2,1,0:T(8,128)} %sol_in.1) | copy-start | bytes 786436

commit v6 on v5

--- a/solution.py
+++ b/solution.py
@@ -32,10 +32,15 @@
     return dot(ah, bh) + (dot(ah, bl) + dot(al, bh))
 
 
+def fold(x):
+    parts = [
+        x[r : r + 8, c : c + LANES] for r in range(0, x.shape[0], 8) for c in range(0, x.shape[1], LANES)
+    ]
+    return functools.reduce(jnp.add, parts)
+
+
 def total(x):
-    rows = jnp.sum(x, axis=0, keepdims=True)
-    n = rows.shape[1] // LANES
-    return functools.reduce(jnp.add, [rows[:, i * LANES : (i + 1) * LANES] for i in range(n)])
+    return jnp.sum(jnp.sum(x, axis=0, keepdims=True), axis=1, keepdims=True)
 
 
 def interleave(a, b):
@@ -421,8 +426,8 @@
         zz = first + i
         return zz, remote(fin.at[i], image.at[odd], fs.at[i], fr.at[odd], on_line(sp, zz, core))
 
-    def add_line(i):
-        zz, cp = home(i)
+    def add_line(i, sums):
+        zz = first + i
         v = tot[zz]
         for k in range(1, NX):
             t = around(lp + k)
@@ -436,9 +441,8 @@
         v = v + local_in[i]
         for p in range(2):
             a, r = v[p], xall[2 * zz + core, p]
-            ps1_s[0:1, :] += total(r * r)
-            ps1_s[1:2, :] += total(r * a)
-            ps1_s[2:3, :] += total(a * a)
+            for k, term in enumerate((r * r, r * a, a * a)):
+                sums[k] = sums[k] + fold(term)
         here = jnp.logical_and(sp == lp, zz == z)
 
         @pl.when(here)
@@ -448,7 +452,6 @@
         @pl.when(jnp.logical_not(here))
         def _():
             fin[i] = v
-            cp.start()
 
     def block_at(i):
         return rows_at(2 + i - (i // 2) * (2 * i - 1))
@@ -474,14 +477,80 @@
             for t in range(per // 2):
                 add_pair(block_at(i - 1) * per // 2 + t)
 
-    ps1_s[...] = jnp.zeros_like(ps1_s)
     loop(0, groups, inverse)
     for t in range(per // 2):
         add_pair(first + t)
+    sums = [jnp.zeros((8, LANES), F32) for _ in range(3)]
     for i in range(nz // NX):
-        add_line(i)
-
-    def exchange(send, recv, ssem, rsem, me, size, where):
+        add_line(i, sums)
+    sums = [total(v) for v in sums]
+    lane = lax.broadcasted_iota(jnp.int32, (1, LANES), 1)
+    ps1_s[...] = jnp.where(lane == 0, sums[0], jnp.where(lane == 1, sums[1], sums[2]))
+
+    def start_home():
+        for i in range(nz // NX):
+            zz, cp = home(i)
+
+            @pl.when(jnp.logical_not(jnp.logical_and(sp == lp, zz == z)))
+            def _():
+                cp.start()
+
+    def wait_home():
+        for i in range(nz // NX):
+            zz, cp = home(i)
+
+            @pl.when(jnp.logical_not(jnp.logical_and(sp == lp, zz == z)))
+            def _():
+                cp.wait_send()
+
+    def wait_sends():
+        for h in halo1 + halo2:
+            h.wait_send()
+        for j in range(slab):
+            @pl.when(moved(j))
+            def _():
+                res_over(j).wait_send()
+
+            @pl.when(jnp.logical_not(from_self(j)))
+            def _():
+                local_over(j).wait_send()
+
+            maps_over(j, pos[j], sib).wait_send()
+            for k, c in steps:
+                @pl.when(hops(j, k))
+                def _():
+                    maps_over(j, around(pos[j] - shift(j) - k), c).wait_send()
+
+            def sent_maps(t):
+                zt, _, cp = pass_on(sbuf.at[0, j], j, t)
+
+                @pl.when(zt != z)
+                def _():
+                    cp.wait_send()
+
+            loop(0, line, sent_maps)
+            zt, cp = forward_res(j)
+
+            @pl.when(zt != z)
+            def _():
+                cp.wait_send()
+
+        for i in range(nz // NX):
+            for k in range(1, NX):
+                hand(2 * (first + i) + core, i, k).wait_send()
+
+        def sent_sums(zz):
+            to_other(zz).wait_send()
+            to_sib(zz).wait_send()
+            t, cp = to_adder(zz)
+
+            @pl.when(t != lp)
+            def _():
+                cp.wait_send()
+
+        loop(0, nz, sent_sums)
+
+    def exchange(send, recv, ssem, rsem, me, size, where, meanwhile):
         recv[me] = send[...]
 
         def go(k):
@@ -489,13 +558,15 @@
             remote(send, recv.at[me], ssem, rsem, where(t)).start()
 
         loop(1, size, go)
+        for f in meanwhile:
+            f()
         others = recv.at[pl.ds(0, size - 1)]
         remote(others, others, ssem, rsem, where(lax.rem(me + 1, size))).wait_recv()
         return functools.reduce(jnp.add, [recv[i] for i in range(size)])
 
-    ps2_s[...] = exchange(ps1_s, ps1, p1s, p1r, y, n, at_y)
-    sums = jnp.sum(exchange(ps2_s, ps2, p2s, p2r, w, m, at_z), axis=1, keepdims=True)
-    norm_old, curvature, applied2 = sums[0:1], sums[1:2], sums[2:3]
+    ps2_s[...] = exchange(ps1_s, ps1, p1s, p1r, y, n, at_y, (start_home, wait_sends))
+    sums = exchange(ps2_s, ps2, p2s, p2r, w, m, at_z, (wait_home,))
+    norm_old, curvature, applied2 = sums[:, 0:1], sums[:, 1:2], sums[:, 2:3]
     alpha = norm_old / curvature
     norm_new = jnp.maximum(alpha * alpha * applied2 - norm_old, 0.0)
     out_alpha[...] = jnp.broadcast_to(alpha, (1, cols))
@@ -512,56 +583,6 @@
     for recv, ssem, rsem, size, there in ((ps1, p1s, p1r, n, at_y(up_y)), (ps2, p2s, p2r, m, at_z(up_z))):
         others = recv.at[pl.ds(0, size - 1)]
         remote(others, others, ssem, rsem, there).wait_send()
-    for h in halo1 + halo2:
-        h.wait_send()
-    for j in range(slab):
-        @pl.when(moved(j))
-        def _():
-            res_over(j).wait_send()
-
-        @pl.when(jnp.logical_not(from_self(j)))
-        def _():
-            local_over(j).wait_send()
-
-        maps_over(j, pos[j], sib).wait_send()
-        for k, c in steps:
-            @pl.when(hops(j, k))
-            def _():
-                maps_over(j, around(pos[j] - shift(j) - k), c).wait_send()
-
-        def sent_maps(t):
-            zt, _, cp = pass_on(sbuf.at[0, j], j, t)
-
-            @pl.when(zt != z)
-            def _():
-                cp.wait_send()
-
-        loop(0, line, sent_maps)
-        zt, cp = forward_res(j)
-
-        @pl.when(zt != z)
-        def _():
-            cp.wait_send()
-
-    for i in range(nz // NX):
-        for k in range(1, NX):
-            hand(2 * (first + i) + core, i, k).wait_send()
-        zz, cp = home(i)
-
-        @pl.when(jnp.logical_not(jnp.logical_and(sp == lp, zz == z)))
-        def _():
-            cp.wait_send()
-
-    def sent_sums(zz):
-        to_other(zz).wait_send()
-        to_sib(zz).wait_send()
-        t, cp = to_adder(zz)
-
-        @pl.when(t != lp)
-        def _():
-            cp.wait_send()
-
-    loop(0, nz, sent_sums)
 
 
 def matrix(length, rows):
@@ -606,7 +627,7 @@
             f32(n, *chunk), f32(n // 2, *chunk), f32(n // 2, *chunk), f32(n // 2 // NX, NX, *chunk), f32(2, *chunk),
             f32(slab, *chunk), f32(*solution.shape), f32(slab, *chunk), f32(n // 2 // NX, *chunk),
             f32(2, *chunk), f32(8, cols), f32(8, cols), f32(*chunk), f32(*chunk), f32(8, cols), f32(8, cols),
-            f32(8, LANES), f32(n, 8, LANES), f32(8, LANES), f32(m, 8, LANES),
+            f32(1, LANES), f32(n, 1, LANES), f32(1, LANES), f32(m, 1, LANES),
             dma((5,)), dma((2 * NX * slab,)), dma((2 * NX * slab,)), dma((2 * NX * slab,)), dma((n,)), dma((slab,)), dma((slab,)),
             dma((slab,)), dma((n,)), dma((n // 2 // NX * NX,)), dma((n // 2,)),
             dma((n // 2,)), dma((n // 2,)), dma((n // 2,)), dma((n // 2,)), dma((n // 2 // NX,)), dma((slab,)),

time: 120 us -> 116 us (0.967)
  Pallas kernels: 117 us -> 113 us
    pallas_call x1, Pallas kernels: 117 us -> 113 us  [body(): pl.pallas_call(functools.partial(kernel, n, m), out_shape=(jax.ShapeDtype...]
where the time goes in v6:
time: 116 us
  Pallas kernels  113 us (97%)
  other arithmetic  1.92 us (2%)
    pallas_call x1, Pallas kernels, body(): pl.pallas_call(functools.partial(kernel, n, m), out_shape=(jax.ShapeDtype...  113 us

profile of v6, /device:TPU:1, one launch (start us, length us, event | category | flops | bytes accessed | tf_op | source)
XLA Modules:
  0.0 115.5 jit_solution(17150195648565181284)
XLA Ops:
  0.6 0.0 copy-start
  0.6 0.0 copy-start.1
  0.7 112.9 %iteration.1 = (f32[2,2,32,512]{3,2,1,0:T(8,128)}, f32[1,512]{1,0:T(1,128)}, f32[1,512]{1,0:T(1,128)}) custom-call(f32[2,2,32,512]{3,2,1,0:T(8,128)} %sol_in.1, f32[2,2,32,512]{3,2,1,0:T(8,128)} %res_in.1, bf16[2,8,2,32,512]{4,3,2,1,0:T(8,128)(2,1)} %sens_in.1, s32[512,512]{1,0:T(8,128)} %samp_in.1, bf16[2,1024,1024]{2,1,0:T(8,128)(2,1)} %constant.2.clone.g_in), custom_call_target="tpu_custom_call" | custom-call | tf_op jit(solution)/shard_map/iteration/pallas_call | solution.py:617
  113.6 0.0 copy-done
  113.6 0.0 copy-done.1
  113.6 1.9 %multiply_add_fusion = (f32[2,2,32,512]{3,2,1,0:T(8,128)}, f32[2,2,32,512]{3,2,1,0:T(8,128)}, f32[2,2,32,512]{3,2,1,0:T(8,128)}) fusion(f32[2,2,32,512]{3,2,1,0:T(8,128)S(1)} %copy-done, f32[512]{0:T(512)} %bitcast.3, f32[2,2,32,512]{3,2,1,0:T(8,128)} %get-tuple-element.7, f32[512]{0:T(512)} %bitcast.2, f32[2,2,32,512]{3,2,1,0:T(8,128)S(1)} %copy-done.1), kind=kLoop, calls=%fused_computation | loop fusion | flops 393216 | bytes 1576960 | tf_op jit(solution)/shard_map/add | solution.py:643
Async XLA Ops:
  0.6 112.9 %copy-start = (f32[2,2,32,512]{3,2,1,0:T(8,128)S(1)}, f32[2,2,32,512]{3,2,1,0:T(8,128)}, u32[]{:S(2)}) copy-start(f32[2,2,32,512]{3,2,1,0:T(8,128)} %res_in.1) | copy-start | bytes 786436
  0.6 112.9 %copy-start.1 = (f32[2,2,32,512]{3,2,1,0:T(8,128)S(1)}, f32[2,2,32,512]{3,2,1,0:T(8,128)}, u32[]{:S(2)}) copy-start(f32[2,2,32,512]{3,2,1,0:T(8,128)} %sol_in.1) | copy-start | bytes 786436

commit v7 on v6

--- a/solution.py
+++ b/solution.py
@@ -175,10 +175,19 @@
         me = 2 * pos[j] + core
         return remote(sbuf.at[t, j], relay.at[j, me], xls.at[line * j + t], xlr.at[line * j + me], dev(j, p, z, c))
 
-    for j in range(slab):
-        t = 2 * pos[j] + core
-        forward_maps(sbuf.at[t, j], j, t)
-        maps_over(j, pos[j], sib).start()
+    def hops(j, k):
+        return around(shift(j) + k) != 0
+
+    def send_step(k):
+        for j in range(slab):
+            @pl.when(hops(j, k))
+            def _():
+                maps_over(j, around(pos[j] - shift(j) - k), core).start()
+
+        for j in range(slab):
+            maps_over(j, around(pos[j] - shift(j) - k), sib).start()
+
+    send_step(0)
 
     def moved(j):
         return around(shift(j)) != 0
@@ -194,33 +203,33 @@
         @pl.when(jnp.logical_not(moved(j)))
         def _():
             xrel[j] = res[:, j]
-
-    steps = [(k, c) for k in range(NX) for c in (core, sib)]
-
-    def hops(j, k):
-        return around(shift(j) + k) != 0
-
-    for k, c in steps:
-        for j in range(slab):
-            @pl.when(hops(j, k))
-            def _():
-                maps_over(j, around(pos[j] - shift(j) - k), c).start()
 
     halo1 = [
         remote(sol.at[:, 0], hz.at[0], hs.at[0], hr.at[0], at_z(down_z)),
         remote(res.at[:, 0], hz.at[1], hs.at[1], hr.at[1], at_z(down_z)),
         remote(hy_s, hy, hs.at[2], hr.at[2], at_y(down_y)),
     ]
-    for h in halo1:
-        h.start()
-
     def relay_maps(j, p, c):
         t = 2 * p + c
         remote(sbuf.at[t, j], relay.at[j, t], xls.at[line * j + t], xlr.at[line * j + t], dev(j, p, z, c)).wait_recv()
         forward_maps(relay.at[j, t], j, t)
 
-    for j in range(slab):
-        relay_maps(j, pos[j], sib)
+    def relay_step(k):
+        for j in range(slab):
+            @pl.when(hops(j, k))
+            def _():
+                relay_maps(j, around(pos[j] + shift(j) + k), core)
+
+            @pl.when(jnp.logical_not(hops(j, k)))
+            def _():
+                t = 2 * pos[j] + core
+                forward_maps(sbuf.at[t, j], j, t)
+
+        for j in range(slab):
+            relay_maps(j, around(pos[j] + shift(j) + k), sib)
+
+    relay_step(0)
+    send_step(1)
 
     def forward_res(j):
         zt = slab * around(pos[j] + shift(j)) + j
@@ -241,11 +250,10 @@
         def _():
             xall[y] = xrel[j]
 
-    for k, c in steps:
-        for j in range(slab):
-            @pl.when(hops(j, k))
-            def _():
-                relay_maps(j, around(pos[j] + shift(j) + k), c)
+    for h in halo1:
+        h.start()
+    relay_step(1)
+    send_step(2)
 
     first = 2 * rows_at(0)
 
@@ -268,6 +276,11 @@
         for k in range(1, NX):
             hand(slot, i, k).start()
         to_other(zz).start()
+
+    for k in range(2, NX):
+        relay_step(k)
+        if k + 1 < NX:
+            send_step(k + 1)
 
     for h in halo1:
         h.wait_recv()
@@ -515,11 +528,12 @@
             def _():
                 local_over(j).wait_send()
 
-            maps_over(j, pos[j], sib).wait_send()
-            for k, c in steps:
+            for k in range(NX):
                 @pl.when(hops(j, k))
                 def _():
-                    maps_over(j, around(pos[j] - shift(j) - k), c).wait_send()
+                    maps_over(j, around(pos[j] - shift(j) - k), core).wait_send()
+
+                maps_over(j, around(pos[j] - shift(j) - k), sib).wait_send()
 
             def sent_maps(t):
                 zt, _, cp = pass_on(sbuf.at[0, j], j, t)

time: 116 us -> 130 us (1.12)
  Pallas kernels: 113 us -> 128 us
    pallas_call x1, Pallas kernels: 113 us -> 128 us  [body(): pl.pallas_call(functools.partial(kernel, n, m), out_shape=(jax.ShapeDtype...]
where the time goes in v7:
time: 130 us
  Pallas kernels  128 us (98%)
  other arithmetic  1.92 us (1%)
    pallas_call x1, Pallas kernels, body(): pl.pallas_call(functools.partial(kernel, n, m), out_shape=(jax.ShapeDtype...  128 us

profile of v7, /device:TPU:1, one launch (start us, length us, event | category | flops | bytes accessed | tf_op | source)
XLA Modules:
  0.0 130.2 jit_solution(11697228968501515240)
XLA Ops:
  0.6 0.0 copy-start
  0.6 0.0 copy-start.1
  0.7 127.6 %iteration.1 = (f32[2,2,32,512]{3,2,1,0:T(8,128)}, f32[1,512]{1,0:T(1,128)}, f32[1,512]{1,0:T(1,128)}) custom-call(f32[2,2,32,512]{3,2,1,0:T(8,128)} %sol_in.1, f32[2,2,32,512]{3,2,1,0:T(8,128)} %res_in.1, bf16[2,8,2,32,512]{4,3,2,1,0:T(8,128)(2,1)} %sens_in.1, s32[512,512]{1,0:T(8,128)} %samp_in.1, bf16[2,1024,1024]{2,1,0:T(8,128)(2,1)} %constant.2.clone.g_in), custom_call_target="tpu_custom_call" | custom-call | tf_op jit(solution)/shard_map/iteration/pallas_call | solution.py:631
  128.3 0.0 copy-done
  128.3 0.0 copy-done.1
  128.3 1.9 %multiply_add_fusion = (f32[2,2,32,512]{3,2,1,0:T(8,128)}, f32[2,2,32,512]{3,2,1,0:T(8,128)}, f32[2,2,32,512]{3,2,1,0:T(8,128)}) fusion(f32[2,2,32,512]{3,2,1,0:T(8,128)S(1)} %copy-done, f32[512]{0:T(512)} %bitcast.3, f32[2,2,32,512]{3,2,1,0:T(8,128)} %get-tuple-element.7, f32[512]{0:T(512)} %bitcast.2, f32[2,2,32,512]{3,2,1,0:T(8,128)S(1)} %copy-done.1), kind=kLoop, calls=%fused_computation | loop fusion | flops 393216 | bytes 1576960 | tf_op jit(solution)/shard_map/add | solution.py:657
Async XLA Ops:
  0.6 127.7 %copy-start = (f32[2,2,32,512]{3,2,1,0:T(8,128)S(1)}, f32[2,2,32,512]{3,2,1,0:T(8,128)}, u32[]{:S(2)}) copy-start(f32[2,2,32,512]{3,2,1,0:T(8,128)} %res_in.1) | copy-start | bytes 786436
  0.6 127.7 %copy-start.1 = (f32[2,2,32,512]{3,2,1,0:T(8,128)S(1)}, f32[2,2,32,512]{3,2,1,0:T(8,128)}, u32[]{:S(2)}) copy-start(f32[2,2,32,512]{3,2,1,0:T(8,128)} %sol_in.1) | copy-start | bytes 786436

commit v8 on v6

--- a/solution.py
+++ b/solution.py
@@ -141,86 +141,106 @@
     loads[0].wait()
     loop(0, line, widen)
     loads[1].wait()
-    loads[2].wait()
 
     up_y, down_y = lax.rem(y + 1, n), lax.rem(y + n - 1, n)
     up_z, down_z = lax.rem(w + 1, m), lax.rem(w + m - 1, m)
+    pl.semaphore_wait(barrier, n + m - 2 + slab * NX)
+
+    def pass_on(src, j, t):
+        zt = slab * (t // 2) + j
+        slot = 2 * z + lax.rem(t, 2)
+        cp = remote(src, srecv.at[slot], zs.at[line * j + t], zr.at[z], dev(0, x, zt, core))
+        return zt, slot, cp
+
+    def pass_both(j, p):
+        zt = slab * p + j
+        both = pl.ds(2 * p, 2)
+        cp = remote(relay.at[j, both], srecv.at[pl.ds(2 * z, 2)], zs.at[line * j + 2 * p], zr.at[z], dev(0, x, zt, core))
+        return zt, both, cp
+
+    def forward_maps(src, j, t):
+        zt, slot, cp = pass_on(src, j, t)
+
+        @pl.when(zt != z)
+        def _():
+            cp.start()
+
+        @pl.when(zt == z)
+        def _():
+            srecv[slot] = src[...]
+
+    def maps_over(j, p, c):
+        t = 2 * p + c
+        me = 2 * pos[j] + core
+        return remote(sbuf.at[t, j], relay.at[j, me], xls.at[line * j + t], xlr.at[line * j + me], dev(j, p, z, c))
+
+    for j in range(slab):
+        t = 2 * pos[j] + core
+        forward_maps(sbuf.at[t, j], j, t)
+        maps_over(j, pos[j], sib).start()
+
+    def moved(j):
+        return around(shift(j)) != 0
+
+    def res_over(j):
+        return remote(res.at[:, j], xrel.at[j], xrs.at[j], xrr.at[j], dev(j, around(pos[j] - shift(j)), z, core))
+
+    for j in range(slab):
+        @pl.when(moved(j))
+        def _():
+            res_over(j).start()
+
+        @pl.when(jnp.logical_not(moved(j)))
+        def _():
+            xrel[j] = res[:, j]
+
+    steps = [(k, c) for k in range(NX) for c in (core, sib)]
+
+    def hops(j, k):
+        return around(shift(j) + k) != 0
+
+    for k, c in steps:
+        for j in range(slab):
+            @pl.when(hops(j, k))
+            def _():
+                maps_over(j, around(pos[j] - shift(j) - k), c).start()
+
+    halo1 = [
+        remote(sol.at[:, 0], hz.at[0], hs.at[0], hr.at[0], at_z(down_z)),
+        remote(res.at[:, 0], hz.at[1], hs.at[1], hr.at[1], at_z(down_z)),
+        remote(hy_s, hy, hs.at[2], hr.at[2], at_y(down_y)),
+    ]
+    loads[2].wait()
     for f, field in enumerate((sol, res)):
         for p in range(2):
             for s in range(slab):
                 i = f * 2 * slab + p * slab + s
                 hy_s[i : i + 1, :] = field[p, s, 0:1, :]
 
-    pl.semaphore_wait(barrier, n + m - 2 + slab * NX)
-
-    def pass_on(src, j, t):
-        zt = slab * (t // 2) + j
-        slot = 2 * z + lax.rem(t, 2)
-        cp = remote(src, srecv.at[slot], zs.at[line * j + t], zr.at[slot], dev(0, x, zt, core))
-        return zt, slot, cp
-
-    def forward_maps(src, j, t):
-        zt, slot, cp = pass_on(src, j, t)
-
-        @pl.when(zt != z)
-        def _():
-            cp.start()
-
-        @pl.when(zt == z)
-        def _():
-            srecv[slot] = src[...]
-
-    def maps_over(j, p, c):
-        t = 2 * p + c
-        me = 2 * pos[j] + core
-        return remote(sbuf.at[t, j], relay.at[j, me], xls.at[line * j + t], xlr.at[line * j + me], dev(j, p, z, c))
-
-    for j in range(slab):
-        t = 2 * pos[j] + core
-        forward_maps(sbuf.at[t, j], j, t)
-        maps_over(j, pos[j], sib).start()
-
-    def moved(j):
-        return around(shift(j)) != 0
-
-    def res_over(j):
-        return remote(res.at[:, j], xrel.at[j], xrs.at[j], xrr.at[j], dev(j, around(pos[j] - shift(j)), z, core))
-
-    for j in range(slab):
-        @pl.when(moved(j))
-        def _():
-            res_over(j).start()
-
-        @pl.when(jnp.logical_not(moved(j)))
-        def _():
-            xrel[j] = res[:, j]
-
-    steps = [(k, c) for k in range(NX) for c in (core, sib)]
-
-    def hops(j, k):
-        return around(shift(j) + k) != 0
-
-    for k, c in steps:
-        for j in range(slab):
-            @pl.when(hops(j, k))
-            def _():
-                maps_over(j, around(pos[j] - shift(j) - k), c).start()
-
-    halo1 = [
-        remote(sol.at[:, 0], hz.at[0], hs.at[0], hr.at[0], at_z(down_z)),
-        remote(res.at[:, 0], hz.at[1], hs.at[1], hr.at[1], at_z(down_z)),
-        remote(hy_s, hy, hs.at[2], hr.at[2], at_y(down_y)),
-    ]
     for h in halo1:
         h.start()
 
-    def relay_maps(j, p, c):
+    def got_maps(j, p, c):
         t = 2 * p + c
         remote(sbuf.at[t, j], relay.at[j, t], xls.at[line * j + t], xlr.at[line * j + t], dev(j, p, z, c)).wait_recv()
+
+    def relay_maps(j, p):
+        got_maps(j, p, core)
+        got_maps(j, p, sib)
+        zt, both, cp = pass_both(j, p)
+
+        @pl.when(zt != z)
+        def _():
+            cp.start()
+
+        @pl.when(zt == z)
+        def _():
+            srecv[pl.ds(2 * z, 2)] = relay[j, both]
+
+    for j in range(slab):
+        t = 2 * pos[j] + sib
+        got_maps(j, pos[j], sib)
         forward_maps(relay.at[j, t], j, t)
-
-    for j in range(slab):
-        relay_maps(j, pos[j], sib)
 
     def forward_res(j):
         zt = slab * around(pos[j] + shift(j)) + j
@@ -241,11 +261,11 @@
         def _():
             xall[y] = xrel[j]
 
-    for k, c in steps:
+    for k in range(NX):
         for j in range(slab):
             @pl.when(hops(j, k))
             def _():
-                relay_maps(j, around(pos[j] + shift(j) + k), c)
+                relay_maps(j, around(pos[j] + shift(j) + k))
 
     first = 2 * rows_at(0)
 
@@ -324,16 +344,14 @@
     tile = per * rows
     groups = n // per
 
-    def ready(s):
-        zz = s // 2
-
+    def ready(zz):
         @pl.when(zz != z)
         def _():
-            remote(relay.at[0, 0], srecv.at[s], zs.at[0], zr.at[s], dev(0, x, zz, core)).wait_recv()
-
-        @pl.when(lax.rem(s, 2) == sib)
-        def _():
-            remote(xall.at[s], xall.at[s], os.at[0], xar.at[s], on_line(lp, z, sib)).wait_recv()
+            both = srecv.at[pl.ds(2 * zz, 2)]
+            remote(relay.at[0, pl.ds(0, 2)], both, zs.at[0], zr.at[zz], dev(0, x, zz, core)).wait_recv()
+
+        s = 2 * zz + sib
+        remote(xall.at[s], xall.at[s], os.at[0], xar.at[s], on_line(lp, z, sib)).wait_recv()
 
     at_zero = jnp.full((rows, cols), w, jnp.int32) > 0
     at_top = jnp.logical_and(row == 0, y > 0)
@@ -375,8 +393,8 @@
         def _():
             send_local()
 
-        for t in range(per):
-            ready(q * per + t)
+        for t in range(per // 2):
+            ready(q * per // 2 + t)
         block = []
         for t in range(per):
             sr, si = srecv[q * per + t, 0], srecv[q * per + t, 1]
@@ -454,7 +472,7 @@
             fin[i] = v
 
     def block_at(i):
-        return rows_at(2 + i - (i // 2) * (2 * i - 1))
+        return rows_at(2 - i + (i // 2) * (2 * i - 1) - (i // 3) * 4)
 
     def inverse(i):
         q = block_at(i)
@@ -521,14 +539,20 @@
                 def _():
                     maps_over(j, around(pos[j] - shift(j) - k), c).wait_send()
 
-            def sent_maps(t):
-                zt, _, cp = pass_on(sbuf.at[0, j], j, t)
+            for c in (core, sib):
+                zt, _, cp = pass_on(sbuf.at[0, j], j, 2 * pos[j] + c)
 
                 @pl.when(zt != z)
                 def _():
                     cp.wait_send()
 
-            loop(0, line, sent_maps)
+            for k in range(1, NX):
+                zt, _, cp = pass_both(j, around(pos[j] + k))
+
+                @pl.when(zt != z)
+                def _():
+                    cp.wait_send()
+
             zt, cp = forward_res(j)
 
             @pl.when(zt != z)
@@ -550,22 +574,23 @@
 
         loop(0, nz, sent_sums)
 
-    def exchange(send, recv, ssem, rsem, me, size, where, meanwhile):
+    def exchange(send, recv, ssem, rsem, me, size, where, targets, meanwhile):
         recv[me] = send[...]
 
-        def go(k):
-            t = lax.rem(me + k, size)
+        for t in targets:
             remote(send, recv.at[me], ssem, rsem, where(t)).start()
 
-        loop(1, size, go)
         for f in meanwhile:
             f()
         others = recv.at[pl.ds(0, size - 1)]
         remote(others, others, ssem, rsem, where(lax.rem(me + 1, size))).wait_recv()
         return functools.reduce(jnp.add, [recv[i] for i in range(size)])
 
-    ps2_s[...] = exchange(ps1_s, ps1, p1s, p1r, y, n, at_y, (start_home, wait_sends))
-    sums = exchange(ps2_s, ps2, p2s, p2r, w, m, at_z, (wait_home,))
+    over_z = [2 * lax.rem(z + d, nz) + c for d in (4, 3, 5, 2, 6, 1, 7) for c in (sib, core)] + [2 * z + sib]
+    ways = sorted(((a, b) for a in range(NX) for b in range(NX)), key=lambda d: -min(d[0], NX - d[0]) - min(d[1], NX - d[1]))
+    over_xy = [NX * around(x + a) + around(yy + b) for a, b in ways[:-1]]
+    ps2_s[...] = exchange(ps1_s, ps1, p1s, p1r, y, n, at_y, over_z, (start_home, wait_sends))
+    sums = exchange(ps2_s, ps2, p2s, p2r, w, m, at_z, over_xy, (wait_home,))
     norm_old, curvature, applied2 = sums[:, 0:1], sums[:, 1:2], sums[:, 2:3]
     alpha = norm_old / curvature
     norm_new = jnp.maximum(alpha * alpha * applied2 - norm_old, 0.0)
@@ -628,7 +653,7 @@
             f32(slab, *chunk), f32(*solution.shape), f32(slab, *chunk), f32(n // 2 // NX, *chunk),
             f32(2, *chunk), f32(8, cols), f32(8, cols), f32(*chunk), f32(*chunk), f32(8, cols), f32(8, cols),
             f32(1, LANES), f32(n, 1, LANES), f32(1, LANES), f32(m, 1, LANES),
-            dma((5,)), dma((2 * NX * slab,)), dma((2 * NX * slab,)), dma((2 * NX * slab,)), dma((n,)), dma((slab,)), dma((slab,)),
+            dma((5,)), dma((2 * NX * slab,)), dma((2 * NX * slab,)), dma((2 * NX * slab,)), dma((n // 2,)), dma((slab,)), dma((slab,)),
             dma((slab,)), dma((n,)), dma((n // 2 // NX * NX,)), dma((n // 2,)),
             dma((n // 2,)), dma((n // 2,)), dma((n // 2,)), dma((n // 2,)), dma((n // 2 // NX,)), dma((slab,)),
             dma((5,)), dma((5,)), dma((slab,)), dma((n // 2 // NX,)), dma, dma, dma, dma,

time: 116 us -> 114 us (0.983)
  Pallas kernels: 113 us -> 111 us
    pallas_call x1, Pallas kernels: 113 us -> 111 us  [body(): pl.pallas_call(functools.partial(kernel, n, m), out_shape=(jax.ShapeDtype...]
where the time goes in v8:
time: 114 us
  Pallas kernels  111 us (97%)
  other arithmetic  1.92 us (2%)
    pallas_call x1, Pallas kernels, body(): pl.pallas_call(functools.partial(kernel, n, m), out_shape=(jax.ShapeDtype...  111 us

profile of v8, /device:TPU:1, one launch (start us, length us, event | category | flops | bytes accessed | tf_op | source)
XLA Modules:
  0.0 113.7 jit_solution(13607598300823131627)
XLA Ops:
  0.6 0.0 copy-start
  0.6 0.0 copy-start.1
  0.7 111.1 %iteration.1 = (f32[2,2,32,512]{3,2,1,0:T(8,128)}, f32[1,512]{1,0:T(1,128)}, f32[1,512]{1,0:T(1,128)}) custom-call(f32[2,2,32,512]{3,2,1,0:T(8,128)} %sol_in.1, f32[2,2,32,512]{3,2,1,0:T(8,128)} %res_in.1, bf16[2,8,2,32,512]{4,3,2,1,0:T(8,128)(2,1)} %sens_in.1, s32[512,512]{1,0:T(8,128)} %samp_in.1, bf16[2,1024,1024]{2,1,0:T(8,128)(2,1)} %constant.2.clone.g_in), custom_call_target="tpu_custom_call" | custom-call | tf_op jit(solution)/shard_map/iteration/pallas_call | solution.py:642
  111.8 0.0 copy-done
  111.8 0.0 copy-done.1
  111.8 1.9 %multiply_add_fusion = (f32[2,2,32,512]{3,2,1,0:T(8,128)}, f32[2,2,32,512]{3,2,1,0:T(8,128)}, f32[2,2,32,512]{3,2,1,0:T(8,128)}) fusion(f32[2,2,32,512]{3,2,1,0:T(8,128)S(1)} %copy-done, f32[512]{0:T(512)} %bitcast.3, f32[2,2,32,512]{3,2,1,0:T(8,128)} %get-tuple-element.7, f32[512]{0:T(512)} %bitcast.2, f32[2,2,32,512]{3,2,1,0:T(8,128)S(1)} %copy-done.1), kind=kLoop, calls=%fused_computation | loop fusion | flops 393216 | bytes 1576960 | tf_op jit(solution)/shard_map/add | solution.py:668
Async XLA Ops:
  0.6 111.2 %copy-start = (f32[2,2,32,512]{3,2,1,0:T(8,128)S(1)}, f32[2,2,32,512]{3,2,1,0:T(8,128)}, u32[]{:S(2)}) copy-start(f32[2,2,32,512]{3,2,1,0:T(8,128)} %res_in.1) | copy-start | bytes 786436
  0.6 111.2 %copy-start.1 = (f32[2,2,32,512]{3,2,1,0:T(8,128)S(1)}, f32[2,2,32,512]{3,2,1,0:T(8,128)}, u32[]{:S(2)}) copy-start(f32[2,2,32,512]{3,2,1,0:T(8,128)} %sol_in.1) | copy-start | bytes 786436

commit v9 on v8

--- a/solution.py
+++ b/solution.py
@@ -58,7 +58,7 @@
     n, m, sol_in, res_in, sens_in, samp_in, g_in,
     out_app, out_alpha, out_beta,
     sol, res, sens, sbuf, relay, srecv, xrel, xall, vh, vl, yacc, yh, yl, samp, g,
-    part, pair, tot, gath, fin, image, smooth, local, local_in,
+    part, pair, tot, gath, fin, smooth, local, local_in,
     hz, hy_s, hy, qz_s, qz, qy_s, qy, ps1_s, ps1, ps2_s, ps2,
     csem, xls, xlr, zs, zr, xrs, xrr, xzs, xar, ms, os,
     prs, prr, gs, gr, fs, fr, hs, hr, ls, lr, p1s, p1r, p2s, p2r,
@@ -266,28 +266,6 @@
             @pl.when(hops(j, k))
             def _():
                 relay_maps(j, around(pos[j] + shift(j) + k))
-
-    first = 2 * rows_at(0)
-
-    def hand(slot, i, k):
-        p = around(lp + k)
-        return remote(xall.at[slot], xall.at[slot], ms.at[i * NX + k], xar.at[slot], on_line(p, z, core))
-
-    def to_other(zz):
-        slot = 2 * zz + core
-        return remote(xall.at[slot], xall.at[slot], os.at[zz], xar.at[slot], on_line(lp, z, sib))
-
-    for i in range(nz // NX):
-        zz = first + i
-        slot = 2 * zz + core
-
-        @pl.when(zz != z)
-        def _():
-            remote(xrel.at[0], xall.at[slot], xzs.at[0], xar.at[slot], dev(0, x, zz, core)).wait_recv()
-
-        for k in range(1, NX):
-            hand(slot, i, k).start()
-        to_other(zz).start()
 
     for h in halo1:
         h.wait_recv()
@@ -333,6 +311,28 @@
     for h in halo2:
         h.start()
 
+    first = 2 * rows_at(0)
+
+    def hand(slot, i, k):
+        p = around(lp + k)
+        return remote(xall.at[slot], xall.at[slot], ms.at[i * NX + k], xar.at[slot], on_line(p, z, core))
+
+    def to_other(zz):
+        slot = 2 * zz + core
+        return remote(xall.at[slot], xall.at[slot], os.at[zz], xar.at[slot], on_line(lp, z, sib))
+
+    for i in range(nz // NX):
+        zz = first + i
+        slot = 2 * zz + core
+
+        @pl.when(zz != z)
+        def _():
+            remote(xrel.at[0], xall.at[slot], xzs.at[0], xar.at[slot], dev(0, x, zz, core)).wait_recv()
+
+        for k in range(1, NX):
+            hand(slot, i, k).start()
+        to_other(zz).start()
+
     for k in range(1, NX):
         for i in range(nz // NX):
             zz = 2 * rows_at(k) + i
@@ -442,7 +442,7 @@
 
     def home(i):
         zz = first + i
-        return zz, remote(fin.at[i], image.at[odd], fs.at[i], fr.at[odd], on_line(sp, zz, core))
+        return zz, remote(fin.at[i], out_app.at[:, odd], fs.at[i], fr.at[odd], on_line(sp, zz, core))
 
     def add_line(i, sums):
         zz = first + i
@@ -461,15 +461,7 @@
             a, r = v[p], xall[2 * zz + core, p]
             for k, term in enumerate((r * r, r * a, a * a)):
                 sums[k] = sums[k] + fold(term)
-        here = jnp.logical_and(sp == lp, zz == z)
-
-        @pl.when(here)
-        def _():
-            image[odd] = v
-
-        @pl.when(jnp.logical_not(here))
-        def _():
-            fin[i] = v
+        fin[i] = v
 
     def block_at(i):
         return rows_at(2 - i + (i // 2) * (2 * i - 1) - (i // 3) * 4)
@@ -505,6 +497,9 @@
     lane = lax.broadcasted_iota(jnp.int32, (1, LANES), 1)
     ps1_s[...] = jnp.where(lane == 0, sums[0], jnp.where(lane == 1, sums[1], sums[2]))
 
+    def stay(i):
+        return pltpu.make_async_copy(fin.at[i], out_app.at[:, odd], csem.at[0])
+
     def start_home():
         for i in range(nz // NX):
             zz, cp = home(i)
@@ -513,6 +508,10 @@
             def _():
                 cp.start()
 
+            @pl.when(jnp.logical_and(sp == lp, zz == z))
+            def _():
+                stay(i).start()
+
     def wait_home():
         for i in range(nz // NX):
             zz, cp = home(i)
@@ -520,6 +519,10 @@
             @pl.when(jnp.logical_not(jnp.logical_and(sp == lp, zz == z)))
             def _():
                 cp.wait_send()
+
+            @pl.when(jnp.logical_and(sp == lp, zz == z))
+            def _():
+                stay(i).wait()
 
     def wait_sends():
         for h in halo1 + halo2:
@@ -600,10 +603,7 @@
     for s in range(slab):
         @pl.when(jnp.logical_not(from_self(s)))
         def _():
-            remote(fin.at[0], image.at[s], fs.at[0], fr.at[s], dev(s, around(pos[s] - shift(s)), slab * pos[s] + s, core)).wait_recv()
-
-        for p in range(2):
-            out_app[p, s] = image[s, p]
+            remote(fin.at[0], out_app.at[:, s], fs.at[0], fr.at[s], dev(s, around(pos[s] - shift(s)), slab * pos[s] + s, core)).wait_recv()
 
     for recv, ssem, rsem, size, there in ((ps1, p1s, p1r, n, at_y(up_y)), (ps2, p2s, p2r, m, at_z(up_z))):
         others = recv.at[pl.ds(0, size - 1)]
@@ -643,14 +643,14 @@
         functools.partial(kernel, n, m),
         out_shape=(jax.ShapeDtypeStruct(solution.shape, F32),) + 2 * (jax.ShapeDtypeStruct((1, cols), F32),),
         in_specs=5 * [hbm],
-        out_specs=(vmem, vmem, vmem),
+        out_specs=(hbm, vmem, vmem),
         scratch_shapes=[
             f32(*solution.shape), f32(*residual.shape), bf16(*sensitivity.shape),
             f32(coils, slab, *chunk), f32(slab, 2 * NX, *chunk), f32(n, *chunk), f32(slab, *chunk), f32(n, *chunk),
             bf16(2 * LANES, cols), bf16(2 * LANES, cols), f32(2 * full, cols), bf16(2 * full, cols), bf16(2 * full, cols),
             pltpu.VMEM(sampling.shape, sampling.dtype), bf16(*g.shape),
             f32(n, *chunk), f32(n // 2, *chunk), f32(n // 2, *chunk), f32(n // 2 // NX, NX, *chunk), f32(2, *chunk),
-            f32(slab, *chunk), f32(*solution.shape), f32(slab, *chunk), f32(n // 2 // NX, *chunk),
+            f32(*solution.shape), f32(slab, *chunk), f32(n // 2 // NX, *chunk),
             f32(2, *chunk), f32(8, cols), f32(8, cols), f32(*chunk), f32(*chunk), f32(8, cols), f32(8, cols),
             f32(1, LANES), f32(n, 1, LANES), f32(1, LANES), f32(m, 1, LANES),
             dma((5,)), dma((2 * NX * slab,)), dma((2 * NX * slab,)), dma((2 * NX * slab,)), dma((n // 2,)), dma((slab,)), dma((slab,)),

time: 114 us -> 113 us (level)
  no operation moved by 1% of the time
where the time goes in v9:
time: 113 us
  Pallas kernels  111 us (98%)
  other arithmetic  1.92 us (2%)
    pallas_call x1, Pallas kernels, body(): pl.pallas_call(functools.partial(kernel, n, m), out_shape=(jax.ShapeDtype...  111 us

profile of v9, /device:TPU:1, one launch (start us, length us, event | category | flops | bytes accessed | tf_op | source)
XLA Modules:
  0.0 113.4 jit_solution(10280117208038492837)
XLA Ops:
  0.6 0.0 copy-start
  0.6 0.0 copy-start.1
  0.7 110.8 %iteration.1 = (f32[2,2,32,512]{3,2,1,0:T(8,128)}, f32[1,512]{1,0:T(1,128)}, f32[1,512]{1,0:T(1,128)}) custom-call(f32[2,2,32,512]{3,2,1,0:T(8,128)} %sol_in.1, f32[2,2,32,512]{3,2,1,0:T(8,128)} %res_in.1, bf16[2,8,2,32,512]{4,3,2,1,0:T(8,128)(2,1)} %sens_in.1, s32[512,512]{1,0:T(8,128)} %samp_in.1, bf16[2,1024,1024]{2,1,0:T(8,128)(2,1)} %constant.2.clone.g_in), custom_call_target="tpu_custom_call" | custom-call | tf_op jit(solution)/shard_map/iteration/pallas_call | solution.py:642
  111.4 0.0 copy-done
  111.4 0.0 copy-done.1
  111.4 1.9 %multiply_add_fusion = (f32[2,2,32,512]{3,2,1,0:T(8,128)}, f32[2,2,32,512]{3,2,1,0:T(8,128)}, f32[2,2,32,512]{3,2,1,0:T(8,128)}) fusion(f32[2,2,32,512]{3,2,1,0:T(8,128)S(1)} %copy-done, f32[512]{0:T(512)} %bitcast.3, f32[2,2,32,512]{3,2,1,0:T(8,128)} %get-tuple-element.7, f32[512]{0:T(512)} %bitcast.2, f32[2,2,32,512]{3,2,1,0:T(8,128)S(1)} %copy-done.1), kind=kLoop, calls=%fused_computation | loop fusion | flops 393216 | bytes 1576960 | tf_op jit(solution)/shard_map/add | solution.py:668
Async XLA Ops:
  0.6 110.8 %copy-start = (f32[2,2,32,512]{3,2,1,0:T(8,128)S(1)}, f32[2,2,32,512]{3,2,1,0:T(8,128)}, u32[]{:S(2)}) copy-start(f32[2,2,32,512]{3,2,1,0:T(8,128)} %res_in.1) | copy-start | bytes 786436
  0.6 110.8 %copy-start.1 = (f32[2,2,32,512]{3,2,1,0:T(8,128)S(1)}, f32[2,2,32,512]{3,2,1,0:T(8,128)}, u32[]{:S(2)}) copy-start(f32[2,2,32,512]{3,2,1,0:T(8,128)} %sol_in.1) | copy-start | bytes 786436

commit v10 on v9

--- a/solution.py
+++ b/solution.py
@@ -174,25 +174,25 @@
         me = 2 * pos[j] + core
         return remote(sbuf.at[t, j], relay.at[j, me], xls.at[line * j + t], xlr.at[line * j + me], dev(j, p, z, c))
 
+    def moved(j):
+        return around(shift(j)) != 0
+
+    def res_over(j):
+        return remote(res.at[:, j], xrel.at[j], xrs.at[j], xrr.at[j], dev(j, around(pos[j] - shift(j)), z, core))
+
+    for j in range(slab):
+        @pl.when(moved(j))
+        def _():
+            res_over(j).start()
+
+        @pl.when(jnp.logical_not(moved(j)))
+        def _():
+            xrel[j] = res[:, j]
+
     for j in range(slab):
         t = 2 * pos[j] + core
         forward_maps(sbuf.at[t, j], j, t)
         maps_over(j, pos[j], sib).start()
-
-    def moved(j):
-        return around(shift(j)) != 0
-
-    def res_over(j):
-        return remote(res.at[:, j], xrel.at[j], xrs.at[j], xrr.at[j], dev(j, around(pos[j] - shift(j)), z, core))
-
-    for j in range(slab):
-        @pl.when(moved(j))
-        def _():
-            res_over(j).start()
-
-        @pl.when(jnp.logical_not(moved(j)))
-        def _():
-            xrel[j] = res[:, j]
 
     steps = [(k, c) for k in range(NX) for c in (core, sib)]
 
@@ -237,29 +237,29 @@
         def _():
             srecv[pl.ds(2 * z, 2)] = relay[j, both]
 
+    def forward_res(j):
+        zt = slab * around(pos[j] + shift(j)) + j
+        return zt, remote(xrel.at[j], xall.at[y], xzs.at[j], xar.at[y], dev(0, x, zt, core))
+
+    for j in range(slab):
+        @pl.when(moved(j))
+        def _():
+            res_over(j).wait_recv()
+
+        zt, cp = forward_res(j)
+
+        @pl.when(zt != z)
+        def _():
+            cp.start()
+
+        @pl.when(zt == z)
+        def _():
+            xall[y] = xrel[j]
+
     for j in range(slab):
         t = 2 * pos[j] + sib
         got_maps(j, pos[j], sib)
         forward_maps(relay.at[j, t], j, t)
-
-    def forward_res(j):
-        zt = slab * around(pos[j] + shift(j)) + j
-        return zt, remote(xrel.at[j], xall.at[y], xzs.at[j], xar.at[y], dev(0, x, zt, core))
-
-    for j in range(slab):
-        @pl.when(moved(j))
-        def _():
-            res_over(j).wait_recv()
-
-        zt, cp = forward_res(j)
-
-        @pl.when(zt != z)
-        def _():
-            cp.start()
-
-        @pl.when(zt == z)
-        def _():
-            xall[y] = xrel[j]
 
     for k in range(NX):
         for j in range(slab):

time: 113 us -> 110 us (0.973)
  Pallas kernels: 111 us -> 107 us
    pallas_call x1, Pallas kernels: 111 us -> 107 us  [body(): pl.pallas_call(functools.partial(kernel, n, m), out_shape=(jax.ShapeDtype...]
where the time goes in v10:
time: 110 us
  Pallas kernels  107 us (97%)
  other arithmetic  1.92 us (2%)
    pallas_call x1, Pallas kernels, body(): pl.pallas_call(functools.partial(kernel, n, m), out_shape=(jax.ShapeDtype...  107 us

profile of v10, /device:TPU:1, one launch (start us, length us, event | category | flops | bytes accessed | tf_op | source)
XLA Modules:
  0.0 110.0 jit_solution(10750858586150562717)
XLA Ops:
  0.6 0.0 copy-start
  0.6 0.0 copy-start.1
  0.7 107.4 %iteration.1 = (f32[2,2,32,512]{3,2,1,0:T(8,128)}, f32[1,512]{1,0:T(1,128)}, f32[1,512]{1,0:T(1,128)}) custom-call(f32[2,2,32,512]{3,2,1,0:T(8,128)} %sol_in.1, f32[2,2,32,512]{3,2,1,0:T(8,128)} %res_in.1, bf16[2,8,2,32,512]{4,3,2,1,0:T(8,128)(2,1)} %sens_in.1, s32[512,512]{1,0:T(8,128)} %samp_in.1, bf16[2,1024,1024]{2,1,0:T(8,128)(2,1)} %constant.2.clone.g_in), custom_call_target="tpu_custom_call" | custom-call | tf_op jit(solution)/shard_map/iteration/pallas_call | solution.py:642
  108.1 0.0 copy-done
  108.1 0.0 copy-done.1
  108.1 1.9 %multiply_add_fusion = (f32[2,2,32,512]{3,2,1,0:T(8,128)}, f32[2,2,32,512]{3,2,1,0:T(8,128)}, f32[2,2,32,512]{3,2,1,0:T(8,128)}) fusion(f32[2,2,32,512]{3,2,1,0:T(8,128)S(1)} %copy-done, f32[512]{0:T(512)} %bitcast.3, f32[2,2,32,512]{3,2,1,0:T(8,128)} %get-tuple-element.7, f32[512]{0:T(512)} %bitcast.2, f32[2,2,32,512]{3,2,1,0:T(8,128)S(1)} %copy-done.1), kind=kLoop, calls=%fused_computation | loop fusion | flops 393216 | bytes 1576960 | tf_op jit(solution)/shard_map/add | solution.py:668
Async XLA Ops:
  0.6 107.4 %copy-start = (f32[2,2,32,512]{3,2,1,0:T(8,128)S(1)}, f32[2,2,32,512]{3,2,1,0:T(8,128)}, u32[]{:S(2)}) copy-start(f32[2,2,32,512]{3,2,1,0:T(8,128)} %res_in.1) | copy-start | bytes 786436
  0.6 107.4 %copy-start.1 = (f32[2,2,32,512]{3,2,1,0:T(8,128)S(1)}, f32[2,2,32,512]{3,2,1,0:T(8,128)}, u32[]{:S(2)}) copy-start(f32[2,2,32,512]{3,2,1,0:T(8,128)} %sol_in.1) | copy-start | bytes 786436
